TPU v7x, 256 devices: a whole 4x4x8 slice. The times are simulated.
256 devices in a mesh: tm: 4 (over z_hi), strip: 64 (over z_lo, y, x, core).
Axes of the slice: x: 4, y: 4, z: 8 (z_hi: 4, z_lo: 2; z = z_hi * 2 + z_lo), core: 2. Of those that a mesh axis runs over, the one named last changes fastest.
Arguments:
- density: float32 [4096, 512], P('strip'), may hold values from 0.05 to 0.95
- speed: float32 [4096, 512], P('strip'), may hold values from 0.3 to 1
- codes: int32 [4096, 512], P('strip'), may hold values from 0 to 7
- obstacle: int32 [4096, 512], P('strip'), may hold values 0 or 1
Outputs:
- slice_ends: float32 [4, 4096, 512], P('tm', 'strip')
All inputs are finite; a program needn't handle non-finite values. No bound on the sum of `obstacle` on one device may be relied on, other than what follows from the above.
Results may differ from a plain program's by a relative error of at most 0.00002.
Values sent between devices are 32-bit elements; how exact they have to be, the bound alone decides.
No kernel may reach another device: no remote copies, remote signals or barrier semaphores. Data moves between devices by JAX's collectives and lax.ppermute only.
A program may use at most 64 MiB of HBM per device.

v0:
```python
import jax
import jax.numpy as jnp
from jax import lax
from jax.sharding import PartitionSpec as P

FINE = 8
CSTEPS = 4


OFFSETS = ((0, 1), (-1, 1), (-1, 0), (-1, -1), (0, -1), (1, -1), (1, 0), (1, 1))
LAMBDA = 0.9


def with_halo(block, sides, width):
    for axis, dim in sides:
        count = lax.axis_size(axis)
        forward = [(i, i + 1) for i in range(count - 1)]
        backward = [(target, source) for source, target in forward]
        low = lax.ppermute(
            lax.slice_in_dim(block, block.shape[dim] - width, None, axis=dim), axis, forward
        )
        high = lax.ppermute(lax.slice_in_dim(block, 0, width, axis=dim), axis, backward)
        block = jnp.concatenate([low, block, high], axis=dim)
    return block


def passed_along(block, axis, distance):
    devices = range(lax.axis_size(axis))
    route = [(i - distance, i) for i in devices if i - distance in devices]
    return lax.ppermute(block, axis, route)


def shifted(array, row_step, col_step):
    height, breadth = array.shape
    padded = jnp.pad(array, 1)
    return padded[1 + row_step : 1 + row_step + height, 1 + col_step : 1 + col_step + breadth]


def prepare(indicators, opening):
    count = jnp.zeros_like(opening)
    for d in range(8):
        count = count + shifted(indicators[d] * opening, -OFFSETS[d][0], -OFFSETS[d][1])
    return opening / jnp.maximum(count, 1.0)


def advance(field, push_rate, indicators, weight):
    pushed = push_rate * field
    room = (1.0 - field) * weight
    leaving = jnp.zeros_like(field)
    arriving = jnp.zeros_like(field)
    for d in range(8):
        leaving = leaving + indicators[d] * shifted(room, OFFSETS[d][0], OFFSETS[d][1])
        arriving = arriving + shifted(pushed * indicators[d], -OFFSETS[d][0], -OFFSETS[d][1])
    return field - pushed * leaving + room * arriving


def halve(array):
    return 0.25 * (array[0::2, 0::2] + array[1::2, 0::2] + array[0::2, 1::2] + array[1::2, 1::2])


def double(array):
    return jnp.repeat(jnp.repeat(array, 2, axis=0), 2, axis=1)


def make_level(push_rate, code_field, opening):
    indicators = [(code_field == float(d)).astype(jnp.float32) for d in range(8)]
    return (push_rate, indicators, prepare(indicators, opening))


def window(level, lower, upper):
    push_rate, indicators, weight = level
    return (push_rate[lower:upper], [item[lower:upper] for item in indicators], weight[lower:upper])


def per_device(density, speed, codes, obstacle):
    height = density.shape[0]
    margin = FINE + 2
    half_margin = margin // 2
    half_height = height // 2
    opening = 1.0 - obstacle.astype(jnp.float32)
    push_rate = LAMBDA * speed * opening
    start = density * opening
    stacked = jnp.stack([push_rate, codes.astype(jnp.float32), opening])
    extended = with_halo(stacked, (("strip", 1),), margin)
    fine_level = make_level(extended[0], extended[1], extended[2])
    coarse_level = make_level(halve(extended[0]), extended[1][0::2, 0::2], halve(extended[2]))
    fine_near = window(fine_level, margin - 1, margin + height + 1)
    coarse_near = window(coarse_level, half_margin - 1, half_margin + half_height + 1)

    def coarse_run(field):
        for step in range(CSTEPS):
            grown = with_halo(field, (("strip", 0),), 1)
            field = advance(grown, *coarse_near)[1:-1]
        return field

    first = lax.axis_index("tm") == 0
    slices = lax.axis_size("tm")

    def relay(value):
        return passed_along(value, "tm", 1)

    def opening_turn(j, current_in):
        guess = coarse_run(halve(current_in))
        return jnp.where(first, start, relay(double(guess)))

    current_in = lax.fori_loop(0, slices - 1, opening_turn, start)
    guess = coarse_run(halve(current_in))
    following = double(guess)
    previous = guess
    field = current_in
    for step in range(FINE):
        grown = with_halo(field, (("strip", 0),), 1)
        field = advance(grown, *fine_near)[1:-1]
    refined = field

    def turn(j, current_in, refined=refined, previous=previous):
        guess = coarse_run(halve(current_in))
        return jnp.where(first, start, relay(refined + double(guess - previous)))

    current_in = lax.fori_loop(0, slices - 1, turn, current_in)
    guess = coarse_run(halve(current_in))
    following = refined + double(guess - previous)
    previous = guess
    return following[None]


def solution(mesh):
    in_specs = (P("strip", None), P("strip", None), P("strip", None), P("strip", None))
    out_specs = P("tm", "strip", None)
    return jax.shard_map(
        per_device, mesh=mesh, in_specs=in_specs, out_specs=out_specs, check_vma=False
    )
```

profile of v0, /device:TPU:160, one launch (start us, length us, event | category | flops | bytes accessed | tf_op | source)
XLA Modules:
  0.0 672.4 jit_solution(18331142977500501774)
XLA Ops:
  4.5 7.0 %collective-permute-start.19 = (f32[3,10,512]{2,0,1:T(4,128)S(1)}, f32[3,10,512]{2,0,1:T(4,128)S(1)}, u32[]{:S(2)}, u32[]{:S(2)}) collective-permute-start(f32[3,10,512]{2,0,1:T(4,128)S(1)} %copy.128), channel_id=1, source_target_pairs={{1,0},{2,1},{3,2},{4,3},{5,4},{6,5},{7,6},{8,7},{9,8},{10,9},{11,1... | collective-permute-start | bytes 184328 | tf_op jit(solution)/shard_map/ppermute | solution.py:22
  14.1 7.7 %collective-permute-done.18 = f32[3,10,512]{2,0,1:T(4,128)S(1)} collective-permute-done((f32[3,10,512]{2,0,1:T(4,128)S(1)}, f32[3,10,512]{2,0,1:T(4,128)S(1)}, u32[]{:S(2)}, u32[]{:S(2)}) %collective-permute-start.18) | collective-permute-done | bytes 61472 | tf_op jit(solution)/shard_map/ppermute | solution.py:19
  47.6 183.4 %while.24 = (s32[]{:T(128)}, f32[64,512]{0,1:T(8,128)S(1)}, pred[]{:T(512)}, f32[34,256]{1,0:T(8,128)S(1)}, f32[34,256]{1,0:T(8,128)S(1)}, /*index=5*/f32[34,256...) while((s32[]{:T(128)}, f32[64,512]{0,1:T(8,128)S(1)}, ...), condition=%wide.region_1.2_spmd, body=%wide.region_0.1_spmd.sunk | while | flops 1468930 | bytes 8749558 | solution.py:106
  101.8 7.1 %collective-permute-done.8 = f32[64,512]{0,1:T(8,128)S(1)} collective-permute-done((f32[64,512]{0,1:T(8,128)S(1)}, f32[64,512]{0,1:T(8,128)S(1)}, u32[]{:S(2)}, u32[]{:S(2)}) %collective-permute-start.8) | collective-permute-done | bytes 131104 | tf_op jit(solution)/shard_map/while/body/eval_jaxpr/ppermute | solution.py:30
  161.5 8.4 %collective-permute-done.8 = f32[64,512]{0,1:T(8,128)S(1)} collective-permute-done((f32[64,512]{0,1:T(8,128)S(1)}, f32[64,512]{0,1:T(8,128)S(1)}, u32[]{:S(2)}, u32[]{:S(2)}) %collective-permute-start.8) | collective-permute-done | bytes 131104 | tf_op jit(solution)/shard_map/while/body/eval_jaxpr/ppermute | solution.py:30
  222.5 8.4 %collective-permute-done.8 = f32[64,512]{0,1:T(8,128)S(1)} collective-permute-done((f32[64,512]{0,1:T(8,128)S(1)}, f32[64,512]{0,1:T(8,128)S(1)}, u32[]{:S(2)}, u32[]{:S(2)}) %collective-permute-start.8) | collective-permute-done | bytes 131104 | tf_op jit(solution)/shard_map/while/body/eval_jaxpr/ppermute | solution.py:30
  248.5 7.4 %collective-permute-start.37 = (f32[1,256]{1,0:T(1,128)S(1)}, f32[1,256]{1,0:T(1,128)S(1)}, u32[]{:S(2)}, u32[]{:S(2)}) collective-permute-start(f32[1,256]{1,0:T(1,128)S(1)} %get-tuple-element.899), channel_id=1, source_target_pairs={{1,0},{2,1},{3,2},{4,3},{5,4},{6,5},{7,6},{8,7},{9,8},{10,9},{11,1... | collective-permute-start | bytes 3080 | tf_op jit(solution)/shard_map/ppermute | solution.py:22
  290.9 7.4 %collective-permute-start.23 = (f32[1,512]{0,1:T(8,128)S(1)}, f32[1,512]{0,1:T(8,128)S(1)}, u32[]{:S(2)}, u32[]{:S(2)}) collective-permute-start(f32[1,512]{0,1:T(8,128)S(1)} %get-tuple-element.781), channel_id=1, source_target_pairs={{1,0},{2,1},{3,2},{4,3},{5,4},{6,5},{7,6},{8,7},{9,8},{10,9},{11,1... | collective-permute-start | bytes 6152 | tf_op jit(solution)/shard_map/ppermute | solution.py:22
  301.7 7.9 %collective-permute-start.43 = (f32[1,256]{0,1:T(8,128)S(1)}, f32[1,256]{0,1:T(8,128)S(1)}, u32[]{:S(2)}, u32[]{:S(2)}) collective-permute-start(f32[1,256]{0,1:T(8,128)S(1)} %get-tuple-element.865), channel_id=1, source_target_pairs={{1,0},{2,1},{3,2},{4,3},{5,4},{6,5},{7,6},{8,7},{9,8},{10,9},{11,1... | collective-permute-start | bytes 3080 | tf_op jit(solution)/shard_map/ppermute | solution.py:22
  314.1 7.9 %collective-permute-start.25 = (f32[1,512]{0,1:T(8,128)S(1)}, f32[1,512]{0,1:T(8,128)S(1)}, u32[]{:S(2)}, u32[]{:S(2)}) collective-permute-start(f32[1,512]{0,1:T(8,128)S(1)} %get-tuple-element.772), channel_id=1, source_target_pairs={{1,0},{2,1},{3,2},{4,3},{5,4},{6,5},{7,6},{8,7},{9,8},{10,9},{11,1... | collective-permute-start | bytes 6152 | tf_op jit(solution)/shard_map/ppermute | solution.py:22
  325.8 8.0 %collective-permute-done.24 = f32[1,512]{0,1:T(8,128)S(1)} collective-permute-done((f32[1,512]{0,1:T(8,128)S(1)}, f32[1,512]{0,1:T(8,128)S(1)}, u32[]{:S(2)}, u32[]{:S(2)}) %collective-permute-start.24) | collective-permute-done | bytes 2080 | tf_op jit(solution)/shard_map/ppermute | solution.py:19
  342.2 8.0 %collective-permute-done.26 = f32[1,512]{0,1:T(8,128)S(1)} collective-permute-done((f32[1,512]{0,1:T(8,128)S(1)}, f32[1,512]{0,1:T(8,128)S(1)}, u32[]{:S(2)}, u32[]{:S(2)}) %collective-permute-start.26) | collective-permute-done | bytes 2080 | tf_op jit(solution)/shard_map/ppermute | solution.py:19
  358.6 8.0 %collective-permute-done.28 = f32[1,512]{0,1:T(8,128)S(1)} collective-permute-done((f32[1,512]{0,1:T(8,128)S(1)}, f32[1,512]{0,1:T(8,128)S(1)}, u32[]{:S(2)}, u32[]{:S(2)}) %collective-permute-start.28) | collective-permute-done | bytes 2080 | tf_op jit(solution)/shard_map/ppermute | solution.py:19
  375.0 8.0 %collective-permute-done.30 = f32[1,512]{0,1:T(8,128)S(1)} collective-permute-done((f32[1,512]{0,1:T(8,128)S(1)}, f32[1,512]{0,1:T(8,128)S(1)}, u32[]{:S(2)}, u32[]{:S(2)}) %collective-permute-start.30) | collective-permute-done | bytes 2080 | tf_op jit(solution)/shard_map/ppermute | solution.py:19
  391.5 8.0 %collective-permute-done.32 = f32[1,512]{0,1:T(8,128)S(1)} collective-permute-done((f32[1,512]{0,1:T(8,128)S(1)}, f32[1,512]{0,1:T(8,128)S(1)}, u32[]{:S(2)}, u32[]{:S(2)}) %collective-permute-start.32) | collective-permute-done | bytes 2080 | tf_op jit(solution)/shard_map/ppermute | solution.py:19
  409.0 13.7 %collective-permute-done.34 = f32[1,512]{0,1:T(8,128)} collective-permute-done((f32[1,512]{0,1:T(8,128)}, f32[1,512]{0,1:T(8,128)}, u32[]{:S(2)}, u32[]{:S(2)}) %collective-permute-start.34) | collective-permute-done | bytes 2080 | tf_op jit(solution)/shard_map/ppermute | solution.py:19
  427.4 183.6 %while.25 = (s32[]{:T(128)}, f32[64,512]{0,1:T(8,128)S(1)}, pred[]{:T(512)}, f32[34,256]{1,0:T(8,128)S(1)}, f32[34,256]{1,0:T(8,128)S(1)}, /*index=5*/f32[34,256...) while((s32[]{:T(128)}, f32[64,512]{0,1:T(8,128)S(1)}, ...), condition=%wide.region_3.4_spmd, body=%wide.region_2.3_spmd.sunk | while | flops 1509890 | bytes 9175558 | solution.py:120
  480.0 8.4 %collective-permute-done.17 = f32[64,512]{0,1:T(8,128)S(1)} collective-permute-done((f32[64,512]{0,1:T(8,128)S(1)}, f32[64,512]{0,1:T(8,128)S(1)}, u32[]{:S(2)}, u32[]{:S(2)}) %collective-permute-start.17) | collective-permute-done | bytes 131104 | tf_op jit(solution)/shard_map/while/body/eval_jaxpr/ppermute | solution.py:30
  531.6 7.1 %collective-permute-done.16 = f32[1,256]{1,0:T(1,128)S(1)} collective-permute-done((f32[1,256]{1,0:T(1,128)S(1)}, f32[1,256]{1,0:T(1,128)S(1)}, u32[]{:S(2)}, u32[]{:S(2)}) %collective-permute-start.16) | collective-permute-done | bytes 1056 | tf_op jit(solution)/shard_map/while/body/eval_jaxpr/ppermute | solution.py:19
  541.4 8.4 %collective-permute-done.17 = f32[64,512]{0,1:T(8,128)S(1)} collective-permute-done((f32[64,512]{0,1:T(8,128)S(1)}, f32[64,512]{0,1:T(8,128)S(1)}, u32[]{:S(2)}, u32[]{:S(2)}) %collective-permute-start.17) | collective-permute-done | bytes 131104 | tf_op jit(solution)/shard_map/while/body/eval_jaxpr/ppermute | solution.py:30
  602.5 8.4 %collective-permute-done.17 = f32[64,512]{0,1:T(8,128)S(1)} collective-permute-done((f32[64,512]{0,1:T(8,128)S(1)}, f32[64,512]{0,1:T(8,128)S(1)}, u32[]{:S(2)}, u32[]{:S(2)}) %collective-permute-start.17) | collective-permute-done | bytes 131104 | tf_op jit(solution)/shard_map/while/body/eval_jaxpr/ppermute | solution.py:30
  632.9 7.7 %collective-permute-done.46 = f32[1,256]{0,1:T(8,128)S(1)} collective-permute-done((f32[1,256]{0,1:T(8,128)S(1)}, f32[1,256]{0,1:T(8,128)S(1)}, u32[]{:S(2)}, u32[]{:S(2)}) %collective-permute-start.46) | collective-permute-done | bytes 1056 | tf_op jit(solution)/shard_map/ppermute | solution.py:19
  646.5 8.0 %collective-permute-done.48 = f32[1,256]{0,1:T(8,128)S(1)} collective-permute-done((f32[1,256]{0,1:T(8,128)S(1)}, f32[1,256]{0,1:T(8,128)S(1)}, u32[]{:S(2)}, u32[]{:S(2)}) %collective-permute-start.48) | collective-permute-done | bytes 1056 | tf_op jit(solution)/shard_map/ppermute | solution.py:19
  660.4 8.0 %collective-permute-done.50 = f32[1,256]{0,1:T(8,128)S(1)} collective-permute-done((f32[1,256]{0,1:T(8,128)S(1)}, f32[1,256]{0,1:T(8,128)S(1)}, u32[]{:S(2)}, u32[]{:S(2)}) %collective-permute-start.50) | collective-permute-done | bytes 1056 | tf_op jit(solution)/shard_map/ppermute | solution.py:19
  (585 shorter events, 489.4 us)
Async XLA Ops:
  98.5 10.4 %collective-permute-start.8 = (f32[64,512]{0,1:T(8,128)S(1)}, f32[64,512]{0,1:T(8,128)S(1)}, u32[]{:S(2)}, u32[]{:S(2)}) collective-permute-start(f32[64,512]{0,1:T(8,128)S(1)} %bitcast.88), channel_id=1, source_target_pairs={{0,64},{64,128},{128,192},{1,65},{65,129},{129,193},{2,66},{66,130... | collective-permute-start | bytes 393224 | tf_op jit(solution)/shard_map/while/body/eval_jaxpr/ppermute | solution.py:30
  159.5 10.4 %collective-permute-start.8 = (f32[64,512]{0,1:T(8,128)S(1)}, f32[64,512]{0,1:T(8,128)S(1)}, u32[]{:S(2)}, u32[]{:S(2)}) collective-permute-start(f32[64,512]{0,1:T(8,128)S(1)} %bitcast.88), channel_id=1, source_target_pairs={{0,64},{64,128},{128,192},{1,65},{65,129},{129,193},{2,66},{66,130... | collective-permute-start | bytes 393224 | tf_op jit(solution)/shard_map/while/body/eval_jaxpr/ppermute | solution.py:30
  220.6 10.4 %collective-permute-start.8 = (f32[64,512]{0,1:T(8,128)S(1)}, f32[64,512]{0,1:T(8,128)S(1)}, u32[]{:S(2)}, u32[]{:S(2)}) collective-permute-start(f32[64,512]{0,1:T(8,128)S(1)} %bitcast.88), channel_id=1, source_target_pairs={{0,64},{64,128},{128,192},{1,65},{65,129},{129,193},{2,66},{66,130... | collective-permute-start | bytes 393224 | tf_op jit(solution)/shard_map/while/body/eval_jaxpr/ppermute | solution.py:30
  243.3 43.2 %collective-permute-start.21 = (f32[1,512]{0,1:T(8,128)}, f32[1,512]{0,1:T(8,128)}, u32[]{:S(2)}, u32[]{:S(2)}) collective-permute-start(f32[1,512]{0,1:T(8,128)} %get-tuple-element.790), channel_id=1, source_target_pairs={{1,0},{2,1},{3,2},{4,3},{5,4},{6,5},{7,6},{8,7},{9,8},{10,9},{11,1... | collective-permute-start | bytes 6152 | tf_op jit(solution)/shard_map/ppermute | solution.py:22
  245.2 41.3 %collective-permute-start.20 = (f32[1,512]{0,1:T(8,128)}, f32[1,512]{0,1:T(8,128)}, u32[]{:S(2)}, u32[]{:S(2)}) collective-permute-start(f32[1,512]{0,1:T(8,128)} %get-tuple-element.789), channel_id=1, source_target_pairs={{0,1},{1,2},{2,3},{3,4},{4,5},{5,6},{6,7},{7,8},{8,9},{9,10},{10,1... | collective-permute-start | bytes 6152 | tf_op jit(solution)/shard_map/ppermute | solution.py:19
  248.5 12.3 %collective-permute-start.37 = (f32[1,256]{1,0:T(1,128)S(1)}, f32[1,256]{1,0:T(1,128)S(1)}, u32[]{:S(2)}, u32[]{:S(2)}) collective-permute-start(f32[1,256]{1,0:T(1,128)S(1)} %get-tuple-element.899), channel_id=1, source_target_pairs={{1,0},{2,1},{3,2},{4,3},{5,4},{6,5},{7,6},{8,7},{9,8},{10,9},{11,1... | collective-permute-start | bytes 3080 | tf_op jit(solution)/shard_map/ppermute | solution.py:22
  270.1 10.5 %collective-permute-start.38 = (f32[1,256]{0,1:T(8,128)S(1)}, f32[1,256]{0,1:T(8,128)S(1)}, u32[]{:S(2)}, u32[]{:S(2)}) collective-permute-start(f32[1,256]{0,1:T(8,128)S(1)} %get-tuple-element.882), channel_id=1, source_target_pairs={{0,1},{1,2},{2,3},{3,4},{4,5},{5,6},{6,7},{7,8},{8,9},{9,10},{10,1... | collective-permute-start | bytes 3080 | tf_op jit(solution)/shard_map/ppermute | solution.py:19
  282.0 18.2 %collective-permute-start.41 = (f32[1,256]{0,1:T(8,128)S(1)}, f32[1,256]{0,1:T(8,128)S(1)}, u32[]{:S(2)}, u32[]{:S(2)}) collective-permute-start(f32[1,256]{0,1:T(8,128)S(1)} %get-tuple-element.874), channel_id=1, source_target_pairs={{1,0},{2,1},{3,2},{4,3},{5,4},{6,5},{7,6},{8,7},{9,8},{10,9},{11,1... | collective-permute-start | bytes 3080 | tf_op jit(solution)/shard_map/ppermute | solution.py:22
  284.0 16.2 %collective-permute-start.40 = (f32[1,256]{0,1:T(8,128)S(1)}, f32[1,256]{0,1:T(8,128)S(1)}, u32[]{:S(2)}, u32[]{:S(2)}) collective-permute-start(f32[1,256]{0,1:T(8,128)S(1)} %get-tuple-element.873), channel_id=1, source_target_pairs={{0,1},{1,2},{2,3},{3,4},{4,5},{5,6},{6,7},{7,8},{8,9},{9,10},{10,1... | collective-permute-start | bytes 3080 | tf_op jit(solution)/shard_map/ppermute | solution.py:19
  290.9 20.6 %collective-permute-start.23 = (f32[1,512]{0,1:T(8,128)S(1)}, f32[1,512]{0,1:T(8,128)S(1)}, u32[]{:S(2)}, u32[]{:S(2)}) collective-permute-start(f32[1,512]{0,1:T(8,128)S(1)} %get-tuple-element.781), channel_id=1, source_target_pairs={{1,0},{2,1},{3,2},{4,3},{5,4},{6,5},{7,6},{8,7},{9,8},{10,9},{11,1... | collective-permute-start | bytes 6152 | tf_op jit(solution)/shard_map/ppermute | solution.py:22
  298.2 13.3 %collective-permute-start.22 = (f32[1,512]{0,1:T(8,128)S(1)}, f32[1,512]{0,1:T(8,128)S(1)}, u32[]{:S(2)}, u32[]{:S(2)}) collective-permute-start(f32[1,512]{0,1:T(8,128)S(1)} %get-tuple-element.780), channel_id=1, source_target_pairs={{0,1},{1,2},{2,3},{3,4},{4,5},{5,6},{6,7},{7,8},{8,9},{9,10},{10,1... | collective-permute-start | bytes 6152 | tf_op jit(solution)/shard_map/ppermute | solution.py:19
  301.7 22.4 %collective-permute-start.43 = (f32[1,256]{0,1:T(8,128)S(1)}, f32[1,256]{0,1:T(8,128)S(1)}, u32[]{:S(2)}, u32[]{:S(2)}) collective-permute-start(f32[1,256]{0,1:T(8,128)S(1)} %get-tuple-element.865), channel_id=1, source_target_pairs={{1,0},{2,1},{3,2},{4,3},{5,4},{6,5},{7,6},{8,7},{9,8},{10,9},{11,1... | collective-permute-start | bytes 3080 | tf_op jit(solution)/shard_map/ppermute | solution.py:22
  309.6 14.5 %collective-permute-start.42 = (f32[1,256]{0,1:T(8,128)S(1)}, f32[1,256]{0,1:T(8,128)S(1)}, u32[]{:S(2)}, u32[]{:S(2)}) collective-permute-start(f32[1,256]{0,1:T(8,128)S(1)} %get-tuple-element.864), channel_id=1, source_target_pairs={{0,1},{1,2},{2,3},{3,4},{4,5},{5,6},{6,7},{7,8},{8,9},{9,10},{10,1... | collective-permute-start | bytes 3080 | tf_op jit(solution)/shard_map/ppermute | solution.py:19
  314.1 11.7 %collective-permute-start.25 = (f32[1,512]{0,1:T(8,128)S(1)}, f32[1,512]{0,1:T(8,128)S(1)}, u32[]{:S(2)}, u32[]{:S(2)}) collective-permute-start(f32[1,512]{0,1:T(8,128)S(1)} %get-tuple-element.772), channel_id=1, source_target_pairs={{1,0},{2,1},{3,2},{4,3},{5,4},{6,5},{7,6},{8,7},{9,8},{10,9},{11,1... | collective-permute-start | bytes 6152 | tf_op jit(solution)/shard_map/ppermute | solution.py:22
  321.9 11.9 %collective-permute-start.24 = (f32[1,512]{0,1:T(8,128)S(1)}, f32[1,512]{0,1:T(8,128)S(1)}, u32[]{:S(2)}, u32[]{:S(2)}) collective-permute-start(f32[1,512]{0,1:T(8,128)S(1)} %get-tuple-element.771), channel_id=1, source_target_pairs={{0,1},{1,2},{2,3},{3,4},{4,5},{5,6},{6,7},{7,8},{8,9},{9,10},{10,1... | collective-permute-start | bytes 6152 | tf_op jit(solution)/shard_map/ppermute | solution.py:19
  338.4 11.9 %collective-permute-start.26 = (f32[1,512]{0,1:T(8,128)S(1)}, f32[1,512]{0,1:T(8,128)S(1)}, u32[]{:S(2)}, u32[]{:S(2)}) collective-permute-start(f32[1,512]{0,1:T(8,128)S(1)} %get-tuple-element.762), channel_id=1, source_target_pairs={{0,1},{1,2},{2,3},{3,4},{4,5},{5,6},{6,7},{7,8},{8,9},{9,10},{10,1... | collective-permute-start | bytes 6152 | tf_op jit(solution)/shard_map/ppermute | solution.py:19
  354.8 11.9 %collective-permute-start.28 = (f32[1,512]{0,1:T(8,128)S(1)}, f32[1,512]{0,1:T(8,128)S(1)}, u32[]{:S(2)}, u32[]{:S(2)}) collective-permute-start(f32[1,512]{0,1:T(8,128)S(1)} %get-tuple-element.753), channel_id=1, source_target_pairs={{0,1},{1,2},{2,3},{3,4},{4,5},{5,6},{6,7},{7,8},{8,9},{9,10},{10,1... | collective-permute-start | bytes 6152 | tf_op jit(solution)/shard_map/ppermute | solution.py:19
  371.2 11.9 %collective-permute-start.30 = (f32[1,512]{0,1:T(8,128)S(1)}, f32[1,512]{0,1:T(8,128)S(1)}, u32[]{:S(2)}, u32[]{:S(2)}) collective-permute-start(f32[1,512]{0,1:T(8,128)S(1)} %get-tuple-element.744), channel_id=1, source_target_pairs={{0,1},{1,2},{2,3},{3,4},{4,5},{5,6},{6,7},{7,8},{8,9},{9,10},{10,1... | collective-permute-start | bytes 6152 | tf_op jit(solution)/shard_map/ppermute | solution.py:19
  387.6 11.9 %collective-permute-start.32 = (f32[1,512]{0,1:T(8,128)S(1)}, f32[1,512]{0,1:T(8,128)S(1)}, u32[]{:S(2)}, u32[]{:S(2)}) collective-permute-start(f32[1,512]{0,1:T(8,128)S(1)} %get-tuple-element.735), channel_id=1, source_target_pairs={{0,1},{1,2},{2,3},{3,4},{4,5},{5,6},{6,7},{7,8},{8,9},{9,10},{10,1... | collective-permute-start | bytes 6152 | tf_op jit(solution)/shard_map/ppermute | solution.py:19
  404.8 17.8 %collective-permute-start.34 = (f32[1,512]{0,1:T(8,128)}, f32[1,512]{0,1:T(8,128)}, u32[]{:S(2)}, u32[]{:S(2)}) collective-permute-start(f32[1,512]{0,1:T(8,128)} %get-tuple-element.726), channel_id=1, source_target_pairs={{0,1},{1,2},{2,3},{3,4},{4,5},{5,6},{6,7},{7,8},{8,9},{9,10},{10,1... | collective-permute-start | bytes 6152 | tf_op jit(solution)/shard_map/ppermute | solution.py:19
  478.1 10.4 %collective-permute-start.17 = (f32[64,512]{0,1:T(8,128)S(1)}, f32[64,512]{0,1:T(8,128)S(1)}, u32[]{:S(2)}, u32[]{:S(2)}) collective-permute-start(f32[64,512]{0,1:T(8,128)S(1)} %add.5353), channel_id=1, source_target_pairs={{0,64},{64,128},{128,192},{1,65},{65,129},{129,193},{2,66},{66,130... | collective-permute-start | bytes 393224 | tf_op jit(solution)/shard_map/while/body/eval_jaxpr/ppermute | solution.py:30
  630.2 10.5 %collective-permute-start.46 = (f32[1,256]{0,1:T(8,128)S(1)}, f32[1,256]{0,1:T(8,128)S(1)}, u32[]{:S(2)}, u32[]{:S(2)}) collective-permute-start(f32[1,256]{0,1:T(8,128)S(1)} %get-tuple-element.839), channel_id=1, source_target_pairs={{0,1},{1,2},{2,3},{3,4},{4,5},{5,6},{6,7},{7,8},{8,9},{9,10},{10,1... | collective-permute-start | bytes 3080 | tf_op jit(solution)/shard_map/ppermute | solution.py:19
  644.0 10.5 %collective-permute-start.48 = (f32[1,256]{0,1:T(8,128)S(1)}, f32[1,256]{0,1:T(8,128)S(1)}, u32[]{:S(2)}, u32[]{:S(2)}) collective-permute-start(f32[1,256]{0,1:T(8,128)S(1)} %get-tuple-element.830), channel_id=1, source_target_pairs={{0,1},{1,2},{2,3},{3,4},{4,5},{5,6},{6,7},{7,8},{8,9},{9,10},{10,1... | collective-permute-start | bytes 3080 | tf_op jit(solution)/shard_map/ppermute | solution.py:19
  657.8 10.5 %collective-permute-start.50 = (f32[1,256]{0,1:T(8,128)S(1)}, f32[1,256]{0,1:T(8,128)S(1)}, u32[]{:S(2)}, u32[]{:S(2)}) collective-permute-start(f32[1,256]{0,1:T(8,128)S(1)} %get-tuple-element.821), channel_id=1, source_target_pairs={{0,1},{1,2},{2,3},{3,4},{4,5},{5,6},{6,7},{7,8},{8,9},{9,10},{10,1... | collective-permute-start | bytes 3080 | tf_op jit(solution)/shard_map/ppermute | solution.py:19
  (88 other events, 525.1 us)
where the time goes:
time: 682 us; the launch traced here: 672 us
  waiting for transfers between devices  319 us (47%)
  starting transfers between devices  218 us (32%)
  local copies, waits for them, and re-layouts  84.6 us (12%)
  other arithmetic  46.6 us (7%)
    ppermute x41, waiting for transfers between devices, with_halo(): lax.ppermute(lax.slice_in_dim(block, block.shape[dim] - width, None, axis...  263 us
    ppermute x41, starting transfers between devices, with_halo(): lax.ppermute(lax.slice_in_dim(block, 0, width, axis=dim), axis, backward)  108 us
    ppermute x41, starting transfers between devices, with_halo(): lax.ppermute(lax.slice_in_dim(block, block.shape[dim] - width, None, axis...  96.9 us
    ppermute x6, waiting for transfers between devices, passed_along(): return lax.ppermute(block, axis, route)  49.3 us
    add x36, other arithmetic, advance(): return field - pushed * leaving + room * arriving  20 us
    mul x74, other arithmetic, advance(): pushed * indicators[d]  14.8 us
    slice x10, local copies, waits for them, and re-layouts, halve(): array[1::2, 1::2]  14.6 us
    slice x10, local copies, waits for them, and re-layouts, halve(): array[1::2, 0::2]  14.6 us
  transfers between devices with their start and end apart: 88, of which 49 were waited for; matrix products, arithmetic and copies ran while one was open for 3% of the time, Pallas kernels for 0%

commit v1 on v0

v1 whole, which is shorter than its diff:
```python
import jax
import jax.numpy as jnp
from jax import lax
from jax.experimental import pallas as pl
from jax.experimental.pallas import tpu as pltpu
from jax.sharding import PartitionSpec as P

FINE = 8
CSTEPS = 4
LAMBDA = 0.9
OFFSETS = ((0, 1), (-1, 1), (-1, 0), (-1, -1), (0, -1), (1, -1), (1, 0), (1, 1))

LANES = 128
TILES = 4
HEIGHT = 64
HALO = 32
WINDOW = HEIGHT + 2 * HALO
ROWS_F = WINDOW // 8
ROWS_C = ROWS_F // 2
TILES_C = TILES // 2
SENT = 3 * HALO + 8


def lane_ids():
    return lax.broadcasted_iota(jnp.int32, (8, LANES), 1)


def sublane_ids():
    return lax.broadcasted_iota(jnp.int32, (8, LANES), 0)


def interleave(tiles):
    lane = lane_ids()
    result = []
    for t in range(TILES):
        index = (lane * TILES + t) % LANES
        picked = [jnp.take_along_axis(tile, index, axis=1) for tile in tiles]
        merged = picked[3]
        for j in (2, 1, 0):
            merged = jnp.where(lane < 32 * (j + 1), picked[j], merged)
        result.append(merged)
    return result


def deinterleave(tiles):
    lane = lane_ids()
    part = lane % TILES
    result = []
    for j in range(TILES):
        index = lane // TILES + 32 * j
        picked = [jnp.take_along_axis(tile, index, axis=1) for tile in tiles]
        merged = picked[3]
        for t in (2, 1, 0):
            merged = jnp.where(part == t, picked[t], merged)
        result.append(merged)
    return result


def prep_kernel(density, speed, codes, obstacle, own, to_next, to_prev):
    for block in range(HEIGHT // 8):
        rows = pl.ds(8 * block, 8)
        cols = [pl.ds(LANES * j, LANES) for j in range(TILES)]
        opening = [1.0 - obstacle[rows, c].astype(jnp.float32) for c in cols]
        rate = [LAMBDA * speed[rows, c] * o for c, o in zip(cols, opening)]
        start = [density[rows, c] * o for c, o in zip(cols, opening)]
        code = [codes[rows, c].astype(jnp.float32) for c in cols]
        for field, tiles in enumerate((rate, code, start)):
            for t, value in enumerate(interleave(tiles)):
                own[t, pl.ds(HEIGHT * field + 8 * block, 8), :] = value
                if block < 4:
                    to_prev[t, pl.ds(HALO * field + 8 * block, 8), :] = value
                else:
                    to_next[t, pl.ds(HALO * field + 8 * (block - 4), 8), :] = value
    for t in range(TILES):
        for target in (to_next, to_prev):
            target[t, pl.ds(3 * HALO, 8), :] = jnp.zeros((8, LANES), jnp.float32)
        for place, (field, row) in enumerate(((0, 31), (0, 30), (1, 31), (1, 30))):
            to_next[t, pl.ds(3 * HALO + place, 1), :] = own[t, pl.ds(HEIGHT * field + row, 1), :]
        for place, (field, row) in enumerate(((0, 32), (0, 33), (1, 32), (1, 33))):
            to_prev[t, pl.ds(3 * HALO + 7 - place, 1), :] = own[t, pl.ds(HEIGHT * field + row, 1), :]


def from_left(tile):
    return jnp.where(lane_ids() == 0, 0.0, pltpu.roll(tile, 1, 1))


def from_right(tile):
    return jnp.where(lane_ids() == LANES - 1, 0.0, pltpu.roll(tile, LANES - 1, 1))


def from_above(tile):
    return jnp.where(sublane_ids() == 0, 0.0, pltpu.roll(tile, 1, 0))


def from_below(tile):
    return jnp.where(sublane_ids() == 7, 0.0, pltpu.roll(tile, 7, 0))


def sweep(rows, tiles, code_at, amount_at, emit, outside=()):
    sums = {}

    def add(r, t, value):
        sums[r, t] = sums[r, t] + value if (r, t) in sums else value

    def finish(r):
        add(r, 0, from_left(sums.pop((r, tiles))))
        add(r, tiles - 1, from_right(sums.pop((r, -1))))
        for t in range(tiles):
            emit(r, t, sums.pop((r, t)))

    for r, row_step, codes, amounts in outside:
        for t in range(tiles):
            for d, (dr, dc) in enumerate(OFFSETS):
                if dr == row_step:
                    add(r + dr, t + dc, jnp.where(codes[t] == float(d), amounts[t], 0.0))
    for r in range(rows):
        for t in range(tiles):
            code = code_at(r, t)
            masks = [code == float(d) for d in range(8)]
            kept, flow = amount_at(r, t, masks)
            if kept is not None:
                add(r, t, kept)
            for mask, (dr, dc) in zip(masks, OFFSETS):
                add(r + dr, t + dc, jnp.where(mask, flow, 0.0))
        if r >= 2:
            finish(r - 1)
    for t in range(-1, tiles + 1):
        add(rows - 1, t, from_below(sums.pop((-1, t))))
        add(0, t, from_above(sums.pop((rows, t))))
    finish(rows - 1)
    finish(0)


def advance(rows, tiles, rho, rate, code, weight):
    field, room = {}, {}

    def load(r):
        for t in range(tiles):
            field[r, t] = rho[r * tiles + t]
            room[r, t] = (1.0 - field[r, t]) * weight[r * tiles + t]
        room[r, -1] = from_left(room[r, tiles - 1])
        room[r, tiles] = from_right(room[r, 0])

    load(rows - 1)
    load(0)
    for t in range(-1, tiles + 1):
        room[-1, t] = from_above(room[rows - 1, t])
        room[rows, t] = from_below(room[0, t])

    def amount_at(r, t, masks):
        if t == 0 and r + 1 < rows - 1:
            load(r + 1)
        leaving = room[r + OFFSETS[0][0], t + OFFSETS[0][1]]
        for mask, (dr, dc) in zip(masks[1:], OFFSETS[1:]):
            leaving = jnp.where(mask, room[r + dr, t + dc], leaving)
        flow = rate[r * tiles + t] * field[r, t] * leaving
        return field[r, t] - flow, flow

    def emit(r, t, value):
        rho[r * tiles + t] = value

    sweep(rows, tiles, lambda r, t: code[r * tiles + t], amount_at, emit)


def fine_at(r, t):
    return r * TILES + t


def coarse_at(r, t):
    return r * TILES_C + t


def halved(get):
    return [
        0.25 * (((get(2 * r, 2 * t) + get(2 * r + 1, 2 * t)) + get(2 * r, 2 * t + 1)) + get(2 * r + 1, 2 * t + 1))
        for r in range(ROWS_C)
        for t in range(TILES_C)
    ]


def main_kernel(
    own, low, high, out, win, ext, rate, code, weight, rho, crate, ccode, cweight, guess, fresh, sems
):
    copies = []

    def copy(source, target):
        copies.append(pltpu.make_async_copy(source, target, sems.at[len(copies)]))
        copies[-1].start()

    for field in range(3):
        copy(low.at[:, pl.ds(HALO * field, HALO), :], win.at[field, :, pl.ds(0, HALO), :])
        copy(own.at[:, pl.ds(HEIGHT * field, HEIGHT), :], win.at[field, :, pl.ds(HALO, HEIGHT), :])
        copy(high.at[:, pl.ds(HALO * field, HALO), :], win.at[field, :, pl.ds(HALO + HEIGHT, HALO), :])
    copy(low.at[:, pl.ds(3 * HALO, 8), :], ext.at[0])
    copy(high.at[:, pl.ds(3 * HALO, 8), :], ext.at[1])
    for item in copies:
        item.wait()

    for r in range(ROWS_F):
        for t in range(TILES):
            rows = pl.ds(r, 8, stride=ROWS_F)
            rate[fine_at(r, t)] = win[0, t, rows, :]
            code[fine_at(r, t)] = win[1, t, rows, :]
            rho[fine_at(r, t)] = win[2, t, rows, :]

    def is_open(value):
        return jnp.where(value > 0.0, 1.0, 0.0)

    def weigh(target, index):
        def emit(r, t, count):
            target[index(r, t)] = target[index(r, t)] / jnp.maximum(count, 1.0)

        return emit

    for i in range(ROWS_F * TILES):
        weight[i] = is_open(rate[i])
    for i, value in enumerate(halved(lambda r, t: weight[fine_at(r, t)])):
        cweight[i] = value
    for i, value in enumerate(halved(lambda r, t: rate[fine_at(r, t)])):
        crate[i] = value
    for r in range(ROWS_C):
        for t in range(TILES_C):
            ccode[coarse_at(r, t)] = code[fine_at(2 * r, 2 * t)]

    fine_out, coarse_out = [], []
    for side, (edge, step, last_f, last_c) in enumerate(((0, 1, -1, -1), (7, -1, ROWS_F, ROWS_C))):
        at_edge = sublane_ids() == edge
        turn = (lambda x, n: pltpu.roll(x, (8 - n) % 8, 0)) if side == 0 else (lambda x, n: pltpu.roll(x, n, 0))
        tile = [ext[side, t] for t in range(TILES)]
        near = [jnp.where(at_edge, is_open(x), 0.0) for x in tile]
        far = [jnp.where(at_edge, is_open(turn(x, 1)), 0.0) for x in tile]
        near_code = [turn(x, 2) for x in tile]
        far_code = [turn(x, 3) for x in tile]
        even_code = far_code if side == 0 else near_code
        mean = [
            0.25 * (((near[2 * t] + far[2 * t]) + near[2 * t + 1]) + far[2 * t + 1]) for t in range(TILES_C)
        ]
        fine_out.append((last_f, step, near_code, near))
        coarse_out.append((last_c, step, [even_code[2 * t] for t in range(TILES_C)], mean))

    sweep(
        ROWS_F, TILES, lambda r, t: code[fine_at(r, t)],
        lambda r, t, masks: (None, is_open(rate[fine_at(r, t)])), weigh(weight, fine_at), fine_out,
    )
    opening_c = [cweight[i] for i in range(ROWS_C * TILES_C)]
    sweep(
        ROWS_C, TILES_C, lambda r, t: ccode[coarse_at(r, t)],
        lambda r, t, masks: (None, opening_c[coarse_at(r, t)]), weigh(cweight, coarse_at), coarse_out,
    )

    n = lax.axis_index("tm")

    def run_fine():
        @pl.loop(0, FINE)
        def _(step):
            advance(ROWS_F, TILES, rho, rate, code, weight)

    def run_coarse(*fields):
        @pl.loop(0, CSTEPS)
        def _(step):
            for item in fields:
                advance(ROWS_C, TILES_C, item, crate, ccode, cweight)

    @pl.when(n > 0)
    def _():
        for i, value in enumerate(halved(lambda r, t: rho[fine_at(r, t)])):
            guess[i] = value
        run_coarse(guess)

    run_fine()
    for i in range(ROWS_C * TILES_C):
        fresh[i] = jnp.zeros((8, LANES), jnp.float32)

    @pl.loop(1, n + 1)
    def _(m):
        for i, value in enumerate(halved(lambda r, t: rho[fine_at(r, t)])):
            fresh[i] = value + fresh[i]
        for r in range(ROWS_F):
            for t in range(TILES):
                rho[fine_at(r, t)] = guess[coarse_at(r // 2, t // 2)]
        run_fine()
        run_coarse(guess, fresh)
        for i in range(ROWS_C * TILES_C):
            fresh[i] = fresh[i] - guess[i]

    for r in range(ROWS_F):
        for t in range(TILES):
            win[0, t, pl.ds(r, 8, stride=ROWS_F), :] = rho[fine_at(r, t)] + fresh[coarse_at(r // 2, t // 2)]
    for block in range(HEIGHT // 8):
        rows = pl.ds(HALO + 8 * block, 8)
        for j, value in enumerate(deinterleave([win[0, t, rows, :] for t in range(TILES)])):
            out[pl.ds(8 * block, 8), pl.ds(LANES * j, LANES)] = value


def per_device(density, speed, codes, obstacle):
    f32 = jnp.float32
    own, to_next, to_prev = pl.pallas_call(
        prep_kernel,
        out_shape=(
            jax.ShapeDtypeStruct((TILES, 3 * HEIGHT, LANES), f32),
            jax.ShapeDtypeStruct((TILES, SENT, LANES), f32),
            jax.ShapeDtypeStruct((TILES, SENT, LANES), f32),
        ),
        name="prep",
    )(density, speed, codes, obstacle)
    count = lax.axis_size("strip")
    forward = [(i, i + 1) for i in range(count - 1)]
    backward = [(target, source) for source, target in forward]
    low = lax.ppermute(to_next, "strip", forward)
    high = lax.ppermute(to_prev, "strip", backward)
    fine = pltpu.VMEM((ROWS_F * TILES, 8, LANES), f32)
    coarse = pltpu.VMEM((ROWS_C * TILES_C, 8, LANES), f32)
    result = pl.pallas_call(
        main_kernel,
        out_shape=jax.ShapeDtypeStruct((HEIGHT, TILES * LANES), f32),
        in_specs=[pl.BlockSpec(memory_space=pl.ANY)] * 3,
        scratch_shapes=[
            pltpu.VMEM((3, TILES, WINDOW, LANES), f32),
            pltpu.VMEM((2, TILES, 8, LANES), f32),
            fine, fine, fine, fine,
            coarse, coarse, coarse, coarse, coarse,
            pltpu.SemaphoreType.DMA((11,)),
        ],
        compiler_params=pltpu.CompilerParams(vmem_limit_bytes=32 * 1024 * 1024),
        name="parareal",
    )(own, low, high)
    return result[None]


def solution(mesh):
    in_specs = (P("strip", None), P("strip", None), P("strip", None), P("strip", None))
    out_specs = P("tm", "strip", None)
    return jax.shard_map(
        per_device, mesh=mesh, in_specs=in_specs, out_specs=out_specs, check_vma=False
    )
```

time: 682 us -> 40.7 us (0.06)
  the two profiles are of different devices: /device:TPU:160 before, /device:TPU:223 now
where the time goes in v1:
time: 40.7 us; the launch traced here: 40.5 us
  Pallas kernels  25.1 us (62%)
  waiting for transfers between devices  9.67 us (24%)
  starting transfers between devices  4.69 us (12%)
  local copies, waits for them, and re-layouts  1 us (2%)
    pallas_call x1, Pallas kernels, per_device(): pl.pallas_call(main_kernel, out_shape=jax.ShapeDtypeStruct((HEIGHT, TILES...  22.3 us
    ppermute x1, waiting for transfers between devices, per_device(): high = lax.ppermute(to_prev, 'strip', backward)  8.51 us
    pallas_call x1, Pallas kernels, per_device(): pl.pallas_call(prep_kernel, out_shape=(jax.ShapeDtypeStruct((TILES, 3 * H...  2.81 us
    ppermute x1, starting transfers between devices, per_device(): low = lax.ppermute(to_next, 'strip', forward)  2.77 us
    ppermute x1, starting transfers between devices, per_device(): high = lax.ppermute(to_prev, 'strip', backward)  1.92 us
    ppermute x1, waiting for transfers between devices, per_device(): low = lax.ppermute(to_next, 'strip', forward)  1.16 us
    unnamed x2, local copies, waits for them, and re-layouts  1 us
  transfers between devices with their start and end apart: 2, of which 2 were waited for; matrix products, arithmetic and copies ran while one was open for 0% of the time, Pallas kernels for 0%

profile of v1, /device:TPU:223, one launch (start us, length us, event | category | flops | bytes accessed | tf_op | source)
XLA Modules:
  0.0 40.5 jit_solution(4349778990229453121)
XLA Ops:
  0.0 2.8 %prep.1 = (f32[4,192,128]{2,1,0:T(8,128)}, f32[4,104,128]{2,1,0:T(8,128)}, f32[4,104,128]{2,1,0:T(8,128)}) custom-call(f32[64,512]{1,0:T(8,128)} %density.1, f32[64,512]{1,0:T(8,128)} %speed.1, s32[64,512]{1,0:T(8,128)} %codes.1, s32[64,512]{1,0:T(8,128)} %obstacle.1), custom_call_target="tpu_custom_call" | custom-call | tf_op jit(solution)/shard_map/prep/pallas_call | solution.py:297
  2.8 2.8 %collective-permute-start = (f32[4,104,128]{2,1,0:T(8,128)}, f32[4,104,128]{2,1,0:T(8,128)S(1)}, u32[]{:S(2)}, u32[]{:S(2)}) collective-permute-start(f32[4,104,128]{2,1,0:T(8,128)} %get-tuple-element.9), channel_id=1, source_target_pairs={{0,1},{1,2},{2,3},{3,4},{4,5},{5,6},{6,7},{7,8},{8,9},{9,10},{10,1... | collective-permute-start | bytes 638984 | tf_op jit(solution)/shard_map/ppermute | solution.py:309
  5.6 1.9 %collective-permute-start.1 = (f32[4,104,128]{2,1,0:T(8,128)}, f32[4,104,128]{2,1,0:T(8,128)S(1)}, u32[]{:S(2)}, u32[]{:S(2)}) collective-permute-start(f32[4,104,128]{2,1,0:T(8,128)} %get-tuple-element.10), channel_id=1, source_target_pairs={{1,0},{2,1},{3,2},{4,3},{5,4},{6,5},{7,6},{8,7},{9,8},{10,9},{11,1... | collective-permute-start | bytes 638984 | tf_op jit(solution)/shard_map/ppermute | solution.py:310
  7.5 1.2 %collective-permute-done.low = f32[4,104,128]{2,1,0:T(8,128)S(1)} collective-permute-done((f32[4,104,128]{2,1,0:T(8,128)}, f32[4,104,128]{2,1,0:T(8,128)S(1)}, u32[]{:S(2)}, u32[]{:S(2)}) %collective-permute-start) | collective-permute-done | bytes 213024 | tf_op jit(solution)/shard_map/ppermute | solution.py:309
  8.7 8.5 %collective-permute-done.1.high = f32[4,104,128]{2,1,0:T(8,128)S(1)} collective-permute-done((f32[4,104,128]{2,1,0:T(8,128)}, f32[4,104,128]{2,1,0:T(8,128)S(1)}, u32[]{:S(2)}, u32[]{:S(2)}) %collective-permute-start.1) | collective-permute-done | bytes 213024 | tf_op jit(solution)/shard_map/ppermute | solution.py:310
  17.2 0.0 copy-start
  17.2 1.0 %copy-done = f32[4,192,128]{2,1,0:T(8,128)S(1)} copy-done((f32[4,192,128]{2,1,0:T(8,128)S(1)}, f32[4,192,128]{2,1,0:T(8,128)}, u32[]{:S(2)}) %copy-start) | copy-done | bytes 393240
  18.2 22.3 %parareal.1 = f32[64,512]{1,0:T(8,128)} custom-call(f32[4,192,128]{2,1,0:T(8,128)S(1)} %copy-done, f32[4,104,128]{2,1,0:T(8,128)S(1)} %collective-permute-done.low, f32[4,104,128]{2,1,0:T(8,128)S(1)} %collective-permute-done.1.high), custom_call_target="tpu_custom_call" | custom-call | tf_op jit(solution)/shard_map/parareal/pallas_call | solution.py:313
Async XLA Ops:
  2.8 5.9 %collective-permute-start = (f32[4,104,128]{2,1,0:T(8,128)}, f32[4,104,128]{2,1,0:T(8,128)S(1)}, u32[]{:S(2)}, u32[]{:S(2)}) collective-permute-start(f32[4,104,128]{2,1,0:T(8,128)} %get-tuple-element.9), channel_id=1, source_target_pairs={{0,1},{1,2},{2,3},{3,4},{4,5},{5,6},{6,7},{7,8},{8,9},{9,10},{10,1... | collective-permute-start | bytes 638984 | tf_op jit(solution)/shard_map/ppermute | solution.py:309
  5.6 11.6 %collective-permute-start.1 = (f32[4,104,128]{2,1,0:T(8,128)}, f32[4,104,128]{2,1,0:T(8,128)S(1)}, u32[]{:S(2)}, u32[]{:S(2)}) collective-permute-start(f32[4,104,128]{2,1,0:T(8,128)} %get-tuple-element.10), channel_id=1, source_target_pairs={{1,0},{2,1},{3,2},{4,3},{5,4},{6,5},{7,6},{8,7},{9,8},{10,9},{11,1... | collective-permute-start | bytes 638984 | tf_op jit(solution)/shard_map/ppermute | solution.py:310
  17.2 1.0 %copy-start = (f32[4,192,128]{2,1,0:T(8,128)S(1)}, f32[4,192,128]{2,1,0:T(8,128)}, u32[]{:S(2)}) copy-start(f32[4,192,128]{2,1,0:T(8,128)} %get-tuple-element.8.own) | copy-start | bytes 1179652

commit v2 on v1

v2 whole, which is shorter than its diff:
```python
import jax
import jax.numpy as jnp
from jax import lax
from jax.experimental import pallas as pl
from jax.experimental.pallas import tpu as pltpu
from jax.sharding import PartitionSpec as P

FINE = 8
CSTEPS = 4
LAMBDA = 0.9
OFFSETS = ((0, 1), (-1, 1), (-1, 0), (-1, -1), (0, -1), (1, -1), (1, 0), (1, 1))

LANES = 128
TILES = 4
TILES_C = TILES // 2
HEIGHT = 64
HALO = 32
MARGIN = 40
SPAN = HEIGHT + 2 * MARGIN
SENT = 3 * HALO + 8
STAGES = ((6, 18), (16, 14), (24, 12), (32, 10))
SPAN_C = 8 * STAGES[0][1] // 2


def lane_ids():
    return lax.broadcasted_iota(jnp.int32, (8, LANES), 1)


def sublane_ids():
    return lax.broadcasted_iota(jnp.int32, (8, LANES), 0)


def interleave(tiles):
    lane = lane_ids()
    result = []
    for t in range(TILES):
        index = (lane * TILES + t) % LANES
        picked = [jnp.take_along_axis(tile, index, axis=1) for tile in tiles]
        merged = picked[3]
        for j in (2, 1, 0):
            merged = jnp.where(lane < 32 * (j + 1), picked[j], merged)
        result.append(merged)
    return result


def deinterleave(tiles):
    lane = lane_ids()
    part = lane % TILES
    result = []
    for j in range(TILES):
        index = lane // TILES + 32 * j
        picked = [jnp.take_along_axis(tile, index, axis=1) for tile in tiles]
        merged = picked[3]
        for t in (2, 1, 0):
            merged = jnp.where(part == t, picked[t], merged)
        result.append(merged)
    return result


def products(density, speed, codes, obstacle, rows):
    cols = [pl.ds(LANES * j, LANES) for j in range(TILES)]
    opening = [1.0 - obstacle[rows, c].astype(jnp.float32) for c in cols]
    rate = [LAMBDA * speed[rows, c] * o for c, o in zip(cols, opening)]
    start = [density[rows, c] * o for c, o in zip(cols, opening)]
    code = [codes[rows, c].astype(jnp.float32) for c in cols]
    return rate, code, start


def edge_tile(rate, code, to_next):
    s = sublane_ids()
    below = jnp.where(s >= 6, rate, pltpu.roll(code, 6, 0))
    above = jnp.where(s < 2, rate, pltpu.roll(code, 2, 0))
    return jnp.where(to_next, below, above)


def cross_kernel(density, speed, codes, obstacle, sent, d_buf, s_buf, c_buf, o_buf, sems):
    odd = lax.axis_index("strip") % 2
    rows = pl.ds(pl.multiple_of(24 * odd, 8), 40)
    bufs = (d_buf, s_buf, c_buf, o_buf)
    copies = [
        pltpu.make_async_copy(source.at[rows, :], buf, sems.at[i])
        for i, (source, buf) in enumerate(zip((density, speed, codes, obstacle), bufs))
    ]
    for item in copies:
        item.start()
    for item in copies:
        item.wait()
    for block in range(4):
        fields = products(*bufs, pl.ds(pl.multiple_of(8 * (block + odd), 8), 8))
        for field, tiles in enumerate(fields):
            for t, value in enumerate(tiles):
                sent[t, pl.ds(HALO * field + 8 * block, 8), :] = value
    rate, code, _ = products(*bufs, pl.ds(pl.multiple_of(32 * (1 - odd), 8), 8))
    for t in range(TILES):
        sent[t, pl.ds(3 * HALO, 8), :] = edge_tile(rate[t], code[t], odd == 1)


def own_kernel(density, speed, codes, obstacle, own, sent):
    even = lax.axis_index("strip") % 2 == 0
    for block in range(HEIGHT // 8):
        fields = products(density, speed, codes, obstacle, pl.ds(8 * block, 8))
        for field, tiles in enumerate(fields):
            for t, value in enumerate(interleave(tiles)):
                own[t, pl.ds(HEIGHT * field + 8 * block, 8), :] = value
    for t in range(TILES):
        for field in range(3):
            for block in range(4):
                first, second = (own[t, pl.ds(HEIGHT * field + 8 * b, 8), :] for b in (block, block + 4))
                sent[t, pl.ds(HALO * field + 8 * block, 8), :] = jnp.where(even, second, first)
        rate, code = (
            jnp.where(even, own[t, pl.ds(HEIGHT * field + 24, 8), :], own[t, pl.ds(HEIGHT * field + 32, 8), :])
            for field in range(2)
        )
        sent[t, pl.ds(3 * HALO, 8), :] = edge_tile(rate, code, even)


def from_left(tile):
    return jnp.where(lane_ids() == 0, 0.0, pltpu.roll(tile, 1, 1))


def from_right(tile):
    return jnp.where(lane_ids() == LANES - 1, 0.0, pltpu.roll(tile, LANES - 1, 1))


def from_above(tile):
    return jnp.where(sublane_ids() == 0, 0.0, pltpu.roll(tile, 1, 0))


def from_below(tile):
    return jnp.where(sublane_ids() == 7, 0.0, pltpu.roll(tile, 7, 0))


def sweep(rows, tiles, amounts_at, emit):
    sums = {}

    def add(r, t, value):
        sums[r, t] = sums[r, t] + value if (r, t) in sums else value

    def finish(r):
        add(r, 0, from_left(sums.pop((r, tiles))))
        add(r, tiles - 1, from_right(sums.pop((r, -1))))
        for t in range(tiles):
            emit(r, t, sums.pop((r, t)))

    for r in range(rows):
        for t in range(tiles):
            kept, flows = amounts_at(r, t)
            if kept is not None:
                add(r, t, kept)
            for flow, (dr, dc) in zip(flows, OFFSETS):
                add(r + dr, t + dc, flow)
        if r >= 2:
            finish(r - 1)
    for t in range(-1, tiles + 1):
        add(rows - 1, t, from_below(sums.pop((-1, t))))
        add(0, t, from_above(sums.pop((rows, t))))
    finish(rows - 1)
    finish(0)


def picked(bits, values):
    for bit in bits:
        values = [jnp.where(bit, odd, even) for even, odd in zip(values[0::2], values[1::2])]
    return values[0]


class Level:
    def __init__(self, first, rows, tiles, rate, parts, bits, weight):
        self.first, self.rows, self.tiles = first, rows, tiles
        self.rate, self.parts, self.bits, self.weight = rate, parts, bits, weight

    def at(self, r, t):
        return r * self.tiles + t

    def cells(self):
        return [(r, t) for r in range(self.rows) for t in range(self.tiles)]

    def line(self, r):
        return pl.ds(self.first + r, 8, stride=self.rows)

    def get(self, ref, r, t):
        return ref[t, self.line(r), :]

    def put(self, ref, r, t, value):
        ref[t, self.line(r), :] = value

    def fill(self, rate_at, code_at, opening_at):
        opening = {}

        def amounts_at(r, t):
            rate, code = rate_at(r, t), code_at(r, t)
            opening[r, t] = opening_at(r, t)
            masks = [code == float(d) for d in range(8)]
            for d, mask in enumerate(masks):
                self.put(self.parts.at[d], r, t, jnp.where(mask, rate, 0.0))
            number = code.astype(jnp.int32)
            for n in range(3):
                self.put(self.bits.at[n], r, t, number & (1 << n))
            return None, [jnp.where(mask, opening[r, t], 0.0) for mask in masks]

        def emit(r, t, count):
            self.put(self.weight, r, t, opening[r, t] / jnp.maximum(count, 1.0))

        sweep(self.rows, self.tiles, amounts_at, emit)

    def advance(self, rho):
        rows, tiles = self.rows, self.tiles
        field, room = {}, {}

        def load(r):
            for t in range(tiles):
                field[r, t] = rho[self.at(r, t)]
                room[r, t] = (1.0 - field[r, t]) * self.get(self.weight, r, t)
            room[r, -1] = from_left(room[r, tiles - 1])
            room[r, tiles] = from_right(room[r, 0])

        load(rows - 1)
        load(0)
        for t in range(-1, tiles + 1):
            room[-1, t] = from_above(room[rows - 1, t])
            room[rows, t] = from_below(room[0, t])

        def amounts_at(r, t):
            if t == 0 and r + 1 < rows - 1:
                load(r + 1)
            bits = [self.get(self.bits.at[n], r, t) != 0 for n in range(3)]
            leaving = picked(bits, [room[r + dr, t + dc] for dr, dc in OFFSETS])
            share = field[r, t] * leaving
            flows = [self.get(self.parts.at[d], r, t) * share for d in range(8)]
            return field[r, t] - self.get(self.rate, r, t) * share, flows

        def emit(r, t, value):
            rho[self.at(r, t)] = value

        sweep(rows, tiles, amounts_at, emit)


def halved(level, get):
    def at(r, t):
        r, t = 2 * r, 2 * t
        return 0.25 * (((get(r, t) + get(r + 1, t)) + get(r, t + 1)) + get(r + 1, t + 1))

    return {(r, t): at(r, t) for r, t in level.cells()}


def is_open(value):
    return jnp.where(value > 0.0, 1.0, 0.0)


def main_kernel(
    own, crossed, paired, out, rate, code, start, parts, bits, weight, rho,
    crate, cparts, cbits, cweight, guess, fresh, last_guess, last_fresh,
):
    even = lax.axis_index("strip") % 2 == 0
    fields = (rate, code, start)
    for i, field in enumerate(fields):
        for t in range(TILES):
            for block in range(HEIGHT // 8):
                field[t, pl.ds(MARGIN + 8 * block, 8), :] = own[t, pl.ds(HEIGHT * i + 8 * block, 8), :]

    zeros = jnp.zeros((8, LANES), jnp.float32)

    def place_halo(tiles_at, high):
        place = pl.multiple_of(jnp.where(high, MARGIN + HEIGHT, MARGIN - HALO), 8)
        beyond = pl.ds(pl.multiple_of(jnp.where(high, SPAN - 8, 0), 8), 8)
        for i, field in enumerate(fields):
            for block in range(HALO // 8):
                for t, tile in enumerate(tiles_at(HALO * i + 8 * block)):
                    field[t, pl.ds(place + 8 * block, 8), :] = tile
        s = sublane_ids()
        for t, tile in enumerate(tiles_at(3 * HALO)):
            there = jnp.where(high, s, 7 - s) < 2
            turned = jnp.where(high, pltpu.roll(tile, 6, 0), pltpu.roll(tile, 2, 0))
            rate[t, beyond, :] = jnp.where(there, tile, 0.0)
            code[t, beyond, :] = jnp.where(there, turned, 0.0)
            start[t, beyond, :] = zeros

    place_halo(lambda row: [paired[t, pl.ds(row, 8), :] for t in range(TILES)], even)
    place_halo(
        lambda row: interleave([crossed[t, pl.ds(row, 8), :] for t in range(TILES)]), jnp.logical_not(even)
    )
    for field in fields:
        for t in range(TILES):
            field[t, pl.ds(SPAN, 8), :] = zeros

    stages = [
        (
            Level(first, rows, TILES, rate, parts, bits, weight),
            Level((first - STAGES[0][0]) // 2, rows // 2, TILES_C, crate, cparts, cbits, cweight),
        )
        for first, rows in STAGES
    ]
    fine, coarse = stages[0]
    rates, openings = {}, {}

    def rate_at(r, t):
        rates[r, t] = fine.get(rate, r, t)
        openings[r, t] = is_open(rates[r, t])
        return rates[r, t]

    fine.fill(rate_at, lambda r, t: fine.get(code, r, t), lambda r, t: openings[r, t])
    mean_rate = halved(coarse, lambda r, t: fine.get(rate, r, t))
    mean_open = halved(coarse, lambda r, t: is_open(fine.get(rate, r, t)))
    for (r, t), value in mean_rate.items():
        coarse.put(crate, r, t, value)
    coarse.fill(
        lambda r, t: mean_rate[r, t], lambda r, t: fine.get(code, 2 * r, 2 * t), lambda r, t: mean_open[r, t]
    )

    n = lax.axis_index("tm")

    def run_fine(level):
        @pl.loop(0, FINE)
        def _(step):
            level.advance(rho)

    def run_coarse(level, *items):
        @pl.loop(0, CSTEPS)
        def _(step):
            for item in items:
                level.advance(item)

    def finish(fine, coarse, change):
        def value(r, t):
            result = rho[fine.at(r, t)]
            return result if change is None else result + change[r // 2, t // 2]

        values = {(r, t): value(r, t) for r, t in fine.cells()}
        for (r, t), item in values.items():
            fine.put(start, r, t, item)
        for (r, t), item in halved(coarse, lambda r, t: values[r, t]).items():
            coarse.put(last_fresh, r, t, item)
            coarse.put(last_guess, r, t, guess[coarse.at(r, t)])

    for r, t in fine.cells():
        rho[fine.at(r, t)] = fine.get(start, r, t)

    @pl.when(n > 0)
    def _():
        for (r, t), value in halved(coarse, lambda r, t: rho[fine.at(r, t)]).items():
            guess[coarse.at(r, t)] = value
        run_coarse(coarse, guess)

    run_fine(fine)
    finish(fine, coarse, None)

    def stage(m):
        fine, coarse = stages[m]

        @pl.when(n >= m)
        def _():
            for r, t in coarse.cells():
                value = coarse.get(last_guess, r, t)
                guess[coarse.at(r, t)] = value
                for i in range(4):
                    rho[fine.at(2 * r + i // 2, 2 * t + i % 2)] = value
                fresh[coarse.at(r, t)] = coarse.get(last_fresh, r, t)
            run_fine(fine)
            run_coarse(coarse, guess, fresh)
            finish(fine, coarse, {(r, t): fresh[coarse.at(r, t)] - guess[coarse.at(r, t)] for r, t in coarse.cells()})

    for m in range(1, len(STAGES)):
        stage(m)

    for block in range(HEIGHT // 8):
        rows = pl.ds(MARGIN + 8 * block, 8)
        for j, value in enumerate(deinterleave([start[t, rows, :] for t in range(TILES)])):
            out[pl.ds(8 * block, 8), pl.ds(LANES * j, LANES)] = value


def per_device(density, speed, codes, obstacle):
    f32, i32 = jnp.float32, jnp.int32
    args = (density, speed, codes, obstacle)
    sent_shape = pltpu.VMEM((TILES, SENT, LANES), f32)
    to_cross = pl.pallas_call(
        cross_kernel,
        out_shape=sent_shape,
        in_specs=[pl.BlockSpec(memory_space=pl.ANY)] * 4,
        scratch_shapes=[pltpu.VMEM((40, TILES * LANES), x.dtype) for x in args] + [pltpu.SemaphoreType.DMA((4,))],
        name="cross",
    )(*args)
    count = lax.axis_size("strip")
    across = [(i, i + 1) for i in range(1, count - 1, 2)]
    within = [(i, i + 1) for i in range(0, count, 2)]
    crossed = lax.ppermute(to_cross, "strip", across + [(j, i) for i, j in across])
    own, to_pair = pl.pallas_call(
        own_kernel,
        out_shape=(pltpu.VMEM((TILES, 3 * HEIGHT, LANES), f32), sent_shape),
        cost_estimate=pl.CostEstimate(flops=10_000_000, bytes_accessed=2_000_000, transcendentals=0),
        name="own",
    )(*args)
    paired = lax.ppermute(to_pair, "strip", within + [(j, i) for i, j in within])

    fine_lines = (TILES, SPAN + 8, LANES)
    coarse_lines = (TILES_C, SPAN_C, LANES)
    fine_cells, coarse_cells = (pltpu.VMEM((SPAN_C * n // 8, 8, LANES), f32) for n in (2 * TILES, TILES_C))
    result = pl.pallas_call(
        main_kernel,
        out_shape=jax.ShapeDtypeStruct((HEIGHT, TILES * LANES), f32),
        in_specs=[pl.BlockSpec(memory_space=pltpu.VMEM)] * 3,
        scratch_shapes=[
            pltpu.VMEM(fine_lines, f32),
            pltpu.VMEM(fine_lines, f32),
            pltpu.VMEM(fine_lines, f32),
            pltpu.VMEM((8, *fine_lines), f32),
            pltpu.VMEM((3, *fine_lines), i32),
            pltpu.VMEM(fine_lines, f32),
            fine_cells,
            pltpu.VMEM(coarse_lines, f32),
            pltpu.VMEM((8, *coarse_lines), f32),
            pltpu.VMEM((3, *coarse_lines), i32),
            pltpu.VMEM(coarse_lines, f32),
            coarse_cells,
            coarse_cells,
            pltpu.VMEM(coarse_lines, f32),
            pltpu.VMEM(coarse_lines, f32),
        ],
        compiler_params=pltpu.CompilerParams(vmem_limit_bytes=32 * 1024 * 1024),
        name="parareal",
    )(own, crossed, paired)
    return result[None]


def solution(mesh):
    in_specs = (P("strip", None), P("strip", None), P("strip", None), P("strip", None))
    out_specs = P("tm", "strip", None)
    return jax.shard_map(
        per_device, mesh=mesh, in_specs=in_specs, out_specs=out_specs, check_vma=False
    )
```

time: 40.7 us -> 27.6 us (0.68)
  Pallas kernels: 25.1 us -> 18 us
  waiting for transfers between devices: 9.67 us -> 6.55 us
  starting transfers between devices: 4.69 us -> 2.94 us
  local copies, waits for them, and re-layouts: 1 us -> 0 us
    pallas_call x1, Pallas kernels: 22.3 us -> 15 us  [per_device(): pl.pallas_call(main_kernel, out_shape=jax.ShapeDtypeStruct((HEIGHT, TILES...]
    ppermute x2, waiting for transfers between devices: 9.67 us -> 6.55 us  [the longest x1 6.54 us: per_device(): lax.ppermute(to_cross, 'strip', across + [(j, i) for i, j in across])]
    ppermute x2, starting transfers between devices: 4.69 us -> 2.94 us  [the longest x1 2.78 us: per_device(): lax.ppermute(to_cross, 'strip', across + [(j, i) for i, j in across])]
    unnamed x2 -> x0, local copies, waits for them, and re-layouts: 1 us -> none
    pallas_call x1 -> x2, Pallas kernels: 2.81 us -> 2.95 us  [the longest x1 1.88 us: per_device(): pl.pallas_call(own_kernel, out_shape=(pltpu.VMEM((TILES, 3 * HEIGHT, LANE...]
  transfers between devices with their start and end apart: 2 -> 2, of which waited for: 2 -> 1; matrix products, arithmetic and copies ran while one was open for 0% -> 0% of each run, Pallas kernels for 0% -> 7%
where the time goes in v2:
time: 27.6 us; the launch traced here: 27.5 us
  Pallas kernels  18 us (65%)
  waiting for transfers between devices  6.55 us (24%)
  starting transfers between devices  2.94 us (11%)
    pallas_call x1, Pallas kernels, per_device(): pl.pallas_call(main_kernel, out_shape=jax.ShapeDtypeStruct((HEIGHT, TILES...  15 us
    ppermute x1, waiting for transfers between devices, per_device(): lax.ppermute(to_cross, 'strip', across + [(j, i) for i, j in across])  6.54 us
    ppermute x1, starting transfers between devices, per_device(): lax.ppermute(to_cross, 'strip', across + [(j, i) for i, j in across])  2.78 us
    pallas_call x1, Pallas kernels, per_device(): pl.pallas_call(own_kernel, out_shape=(pltpu.VMEM((TILES, 3 * HEIGHT, LANE...  1.88 us
    pallas_call x1, Pallas kernels, per_device(): pl.pallas_call(cross_kernel, out_shape=sent_shape, in_specs=[pl.BlockSpec...  1.06 us
  transfers between devices with their start and end apart: 2, of which 1 were waited for; matrix products, arithmetic and copies ran while one was open for 0% of the time, Pallas kernels for 7%

profile of v2, /device:TPU:223, one launch (start us, length us, event | category | flops | bytes accessed | tf_op | source)
XLA Modules:
  0.0 27.5 jit_solution(10457104449634489894)
XLA Ops:
  0.0 1.1 %cross.1 = f32[4,104,128]{2,1,0:T(8,128)S(1)} custom-call(f32[64,512]{1,0:T(8,128)} %density.3, f32[64,512]{1,0:T(8,128)} %speed.3, s32[64,512]{1,0:T(8,128)} %codes.3, s32[64,512]{1,0:T(8,128)} %obstacle.3), custom_call_target="tpu_custom_call" | custom-call | tf_op jit(solution)/shard_map/cross/pallas_call | solution.py:375
  1.1 2.8 %collective-permute-start = (f32[4,104,128]{2,1,0:T(8,128)S(1)}, f32[4,104,128]{2,1,0:T(8,128)S(1)}, u32[]{:S(2)}, u32[]{:S(2)}) collective-permute-start(f32[4,104,128]{2,1,0:T(8,128)S(1)} %cross.1), channel_id=1, source_target_pairs={{1,2},{3,4},{5,6},{7,8},{9,10},{11,12},{13,14},{15,16},{17,18},{19... | collective-permute-start | bytes 638984 | tf_op jit(solution)/shard_map/ppermute | solution.py:385
  3.9 1.9 %own.1 = (f32[4,192,128]{2,1,0:T(8,128)S(1)}, f32[4,104,128]{2,1,0:T(8,128)S(1)}) custom-call(f32[64,512]{1,0:T(8,128)} %density.3, f32[64,512]{1,0:T(8,128)} %speed.3, s32[64,512]{1,0:T(8,128)} %codes.3, s32[64,512]{1,0:T(8,128)} %obstacle.3), custom_call_target="tpu_custom_call" | custom-call | flops 10000000 | bytes 2000000 | tf_op jit(solution)/shard_map/own/pallas_call | solution.py:386
  5.8 0.2 collective-permute-start.1
  5.9 6.5 %collective-permute-done.crossed = f32[4,104,128]{2,1,0:T(8,128)S(1)} collective-permute-done((f32[4,104,128]{2,1,0:T(8,128)S(1)}, f32[4,104,128]{2,1,0:T(8,128)S(1)}, u32[]{:S(2)}, u32[]{:S(2)}) %collective-permute-start) | collective-permute-done | bytes 213024 | tf_op jit(solution)/shard_map/ppermute | solution.py:385
  12.5 0.0 collective-permute-done.1.paired
  12.5 15.0 %parareal.1 = f32[64,512]{1,0:T(8,128)} custom-call(f32[4,192,128]{2,1,0:T(8,128)S(1)} %get-tuple-element.7.own, f32[4,104,128]{2,1,0:T(8,128)S(1)} %collective-permute-done.crossed, f32[4,104,128]{2,1,0:T(8,128)S(1)} %collective-permute-done.1.paired), custom_call_target="tpu_custom_call" | custom-call | tf_op jit(solution)/shard_map/parareal/pallas_call | solution.py:397
Async XLA Ops:
  1.1 11.4 %collective-permute-start = (f32[4,104,128]{2,1,0:T(8,128)S(1)}, f32[4,104,128]{2,1,0:T(8,128)S(1)}, u32[]{:S(2)}, u32[]{:S(2)}) collective-permute-start(f32[4,104,128]{2,1,0:T(8,128)S(1)} %cross.1), channel_id=1, source_target_pairs={{1,2},{3,4},{5,6},{7,8},{9,10},{11,12},{13,14},{15,16},{17,18},{19... | collective-permute-start | bytes 638984 | tf_op jit(solution)/shard_map/ppermute | solution.py:385
  5.8 6.7 %collective-permute-start.1 = (f32[4,104,128]{2,1,0:T(8,128)S(1)}, f32[4,104,128]{2,1,0:T(8,128)S(1)}, u32[]{:S(2)}, u32[]{:S(2)}) collective-permute-start(f32[4,104,128]{2,1,0:T(8,128)S(1)} %get-tuple-element.8), channel_id=1, source_target_pairs={{0,1},{2,3},{4,5},{6,7},{8,9},{10,11},{12,13},{14,15},{16,17},{18,... | collective-permute-start | bytes 638984 | tf_op jit(solution)/shard_map/ppermute | solution.py:392

commit v3 on v2

--- a/solution.py
+++ b/solution.py
@@ -18,8 +18,9 @@
 MARGIN = 40
 SPAN = HEIGHT + 2 * MARGIN
 SENT = 3 * HALO + 8
-STAGES = ((6, 18), (16, 14), (24, 12), (32, 10))
-SPAN_C = 8 * STAGES[0][1] // 2
+STAGES = ((7, 17), (16, 14), (24, 12), (32, 10))
+STAGES_C = ((3, 9), (8, 7), (12, 6), (16, 5))
+SPAN_C = (SPAN + 8) // 2
 
 
 def lane_ids():
@@ -115,11 +116,11 @@
 
 
 def from_left(tile):
-    return jnp.where(lane_ids() == 0, 0.0, pltpu.roll(tile, 1, 1))
+    return pltpu.roll(tile, 1, 1)
 
 
 def from_right(tile):
-    return jnp.where(lane_ids() == LANES - 1, 0.0, pltpu.roll(tile, LANES - 1, 1))
+    return pltpu.roll(tile, LANES - 1, 1)
 
 
 def from_above(tile):
@@ -143,17 +144,20 @@
             emit(r, t, sums.pop((r, t)))
 
     for r in range(rows):
-        for t in range(tiles):
+        for t in (*range(1, tiles - 1), 0, tiles - 1):
             kept, flows = amounts_at(r, t)
             if kept is not None:
                 add(r, t, kept)
             for flow, (dr, dc) in zip(flows, OFFSETS):
                 add(r + dr, t + dc, flow)
+        if r == rows - 1:
+            for t in range(-1, tiles + 1):
+                add(0, t, from_above(sums.pop((rows, t))))
+        if r == 0:
+            for t in range(-1, tiles + 1):
+                add(rows - 1, t, from_below(sums.pop((-1, t))))
         if r >= 2:
             finish(r - 1)
-    for t in range(-1, tiles + 1):
-        add(rows - 1, t, from_below(sums.pop((-1, t))))
-        add(0, t, from_above(sums.pop((rows, t))))
     finish(rows - 1)
     finish(0)
 
@@ -190,7 +194,14 @@
         def amounts_at(r, t):
             rate, code = rate_at(r, t), code_at(r, t)
             opening[r, t] = opening_at(r, t)
+            for side, column_step, lane in ((0, -1, 0), (self.tiles - 1, 1, LANES - 1)):
+                if t == side:
+                    for d, (_, dc) in enumerate(OFFSETS):
+                        if dc == column_step:
+                            code = jnp.where(code == jnp.where(lane_ids() == lane, float(d), -1.0), 8.0, code)
+                    rate = jnp.where(code == 8.0, 0.0, rate)
             masks = [code == float(d) for d in range(8)]
+            self.put(self.rate, r, t, rate)
             for d, mask in enumerate(masks):
                 self.put(self.parts.at[d], r, t, jnp.where(mask, rate, 0.0))
             number = code.astype(jnp.int32)
@@ -203,26 +214,28 @@
 
         sweep(self.rows, self.tiles, amounts_at, emit)
 
-    def advance(self, rho):
+    def advance(self, rho, base=0):
         rows, tiles = self.rows, self.tiles
         field, room = {}, {}
 
         def load(r):
             for t in range(tiles):
-                field[r, t] = rho[self.at(r, t)]
+                field[r, t] = rho[base + self.at(r, t)]
                 room[r, t] = (1.0 - field[r, t]) * self.get(self.weight, r, t)
             room[r, -1] = from_left(room[r, tiles - 1])
             room[r, tiles] = from_right(room[r, 0])
 
-        load(rows - 1)
-        load(0)
-        for t in range(-1, tiles + 1):
-            room[-1, t] = from_above(room[rows - 1, t])
-            room[rows, t] = from_below(room[0, t])
-
         def amounts_at(r, t):
-            if t == 0 and r + 1 < rows - 1:
-                load(r + 1)
+            needed = [row for row in (r - 1, r, r + 1) if 0 <= row < rows] + [rows - 1] * (r == 0)
+            for row in needed:
+                if (row, 0) not in room:
+                    load(row)
+            if r == 0 and (-1, 0) not in room:
+                for tt in range(-1, tiles + 1):
+                    room[-1, tt] = from_above(room[rows - 1, tt])
+            if r == rows - 1 and (rows, 0) not in room:
+                for tt in range(-1, tiles + 1):
+                    room[rows, tt] = from_below(room[0, tt])
             bits = [self.get(self.bits.at[n], r, t) != 0 for n in range(3)]
             leaving = picked(bits, [room[r + dr, t + dc] for dr, dc in OFFSETS])
             share = field[r, t] * leaving
@@ -230,17 +243,20 @@
             return field[r, t] - self.get(self.rate, r, t) * share, flows
 
         def emit(r, t, value):
-            rho[self.at(r, t)] = value
+            rho[base + self.at(r, t)] = value
 
         sweep(rows, tiles, amounts_at, emit)
 
 
-def halved(level, get):
+def halved(coarse, lines, change=lambda tile: tile):
     def at(r, t):
-        r, t = 2 * r, 2 * t
-        return 0.25 * (((get(r, t) + get(r + 1, t)) + get(r, t + 1)) + get(r + 1, t + 1))
-
-    return {(r, t): at(r, t) for r, t in level.cells()}
+        upper, lower = (pl.ds(2 * (coarse.first + r) + i, 8, stride=2 * coarse.rows) for i in range(2))
+        a, b, c, d = (
+            change(lines[2 * t + j, rows, :]) for j, rows in ((0, upper), (0, lower), (1, upper), (1, lower))
+        )
+        return 0.25 * (((a + b) + c) + d)
+
+    return {(r, t): at(r, t) for r, t in coarse.cells()}
 
 
 def is_open(value):
@@ -248,8 +264,8 @@
 
 
 def main_kernel(
-    own, crossed, paired, out, rate, code, start, parts, bits, weight, rho,
-    crate, cparts, cbits, cweight, guess, fresh, last_guess, last_fresh,
+    own, crossed, paired, out, rate, code, start, sending, parts, bits, weight, rho,
+    crate, cparts, cbits, cweight, pair, last_guess, result, sems,
 ):
     even = lax.axis_index("strip") % 2 == 0
     fields = (rate, code, start)
@@ -284,88 +300,95 @@
             field[t, pl.ds(SPAN, 8), :] = zeros
 
     stages = [
-        (
-            Level(first, rows, TILES, rate, parts, bits, weight),
-            Level((first - STAGES[0][0]) // 2, rows // 2, TILES_C, crate, cparts, cbits, cweight),
-        )
-        for first, rows in STAGES
+        (Level(*window, TILES, sending, parts, bits, weight), Level(*window_c, TILES_C, crate, cparts, cbits, cweight))
+        for window, window_c in zip(STAGES, STAGES_C)
     ]
     fine, coarse = stages[0]
-    rates, openings = {}, {}
+    openings = {}
 
     def rate_at(r, t):
-        rates[r, t] = fine.get(rate, r, t)
-        openings[r, t] = is_open(rates[r, t])
-        return rates[r, t]
+        value = fine.get(rate, r, t)
+        openings[r, t] = is_open(value)
+        return value
 
     fine.fill(rate_at, lambda r, t: fine.get(code, r, t), lambda r, t: openings[r, t])
-    mean_rate = halved(coarse, lambda r, t: fine.get(rate, r, t))
-    mean_open = halved(coarse, lambda r, t: is_open(fine.get(rate, r, t)))
-    for (r, t), value in mean_rate.items():
-        coarse.put(crate, r, t, value)
-    coarse.fill(
-        lambda r, t: mean_rate[r, t], lambda r, t: fine.get(code, 2 * r, 2 * t), lambda r, t: mean_open[r, t]
-    )
+    mean_rate = halved(coarse, rate)
+    mean_open = halved(coarse, rate, is_open)
+    def coarse_code_at(r, t):
+        return code[2 * t, pl.ds(2 * (coarse.first + r), 8, stride=2 * coarse.rows), :]
+
+    coarse.fill(lambda r, t: mean_rate[r, t], coarse_code_at, lambda r, t: mean_open[r, t])
 
     n = lax.axis_index("tm")
 
-    def run_fine(level):
-        @pl.loop(0, FINE)
-        def _(step):
-            level.advance(rho)
-
-    def run_coarse(level, *items):
+    half = SPAN_C * TILES_C // 8
+
+    @pl.when(n > 0)
+    def _():
+        for (r, t), value in halved(coarse, start).items():
+            pair[coarse.at(r, t)] = value
+
         @pl.loop(0, CSTEPS)
         def _(step):
-            for item in items:
-                level.advance(item)
-
-    def finish(fine, coarse, change):
-        def value(r, t):
-            result = rho[fine.at(r, t)]
-            return result if change is None else result + change[r // 2, t // 2]
-
-        values = {(r, t): value(r, t) for r, t in fine.cells()}
-        for (r, t), item in values.items():
-            fine.put(start, r, t, item)
-        for (r, t), item in halved(coarse, lambda r, t: values[r, t]).items():
-            coarse.put(last_fresh, r, t, item)
-            coarse.put(last_guess, r, t, guess[coarse.at(r, t)])
+            coarse.advance(pair)
+
+        for r, t in coarse.cells():
+            coarse.put(last_guess, r, t, pair[coarse.at(r, t)])
 
     for r, t in fine.cells():
         rho[fine.at(r, t)] = fine.get(start, r, t)
 
-    @pl.when(n > 0)
-    def _():
-        for (r, t), value in halved(coarse, lambda r, t: rho[fine.at(r, t)]).items():
-            guess[coarse.at(r, t)] = value
-        run_coarse(coarse, guess)
-
-    run_fine(fine)
-    finish(fine, coarse, None)
+    @pl.loop(0, FINE)
+    def _(step):
+        fine.advance(rho)
+
+    for r, t in fine.cells():
+        fine.put(start, r, t, rho[fine.at(r, t)])
 
     def stage(m):
         fine, coarse = stages[m]
 
         @pl.when(n >= m)
         def _():
+            for (r, t), value in halved(coarse, start).items():
+                pair[half + coarse.at(r, t)] = value
             for r, t in coarse.cells():
                 value = coarse.get(last_guess, r, t)
-                guess[coarse.at(r, t)] = value
+                pair[coarse.at(r, t)] = value
                 for i in range(4):
                     rho[fine.at(2 * r + i // 2, 2 * t + i % 2)] = value
-                fresh[coarse.at(r, t)] = coarse.get(last_fresh, r, t)
-            run_fine(fine)
-            run_coarse(coarse, guess, fresh)
-            finish(fine, coarse, {(r, t): fresh[coarse.at(r, t)] - guess[coarse.at(r, t)] for r, t in coarse.cells()})
+
+            @pl.loop(0, FINE)
+            def _(step):
+                fine.advance(rho)
+
+            @pl.loop(0, CSTEPS)
+            def _(step):
+                coarse.advance(pair)
+                coarse.advance(pair, half)
+
+            for r, t in coarse.cells():
+                value = pair[coarse.at(r, t)]
+                change = pair[half + coarse.at(r, t)] - value
+                coarse.put(last_guess, r, t, value)
+                for i in range(4):
+                    rr, tt = 2 * r + i // 2, 2 * t + i % 2
+                    fine.put(start, rr, tt, rho[fine.at(rr, tt)] + change)
 
     for m in range(1, len(STAGES)):
         stage(m)
 
+    copies = []
     for block in range(HEIGHT // 8):
         rows = pl.ds(MARGIN + 8 * block, 8)
         for j, value in enumerate(deinterleave([start[t, rows, :] for t in range(TILES)])):
-            out[pl.ds(8 * block, 8), pl.ds(LANES * j, LANES)] = value
+            result[pl.ds(8 * block, 8), pl.ds(LANES * j, LANES)] = value
+        if block % 2:
+            rows = pl.ds(8 * (block - 1), 16)
+            copies.append(pltpu.make_async_copy(result.at[rows, :], out.at[rows, :], sems.at[block // 2]))
+            copies[-1].start()
+    for item in copies:
+        item.wait()
 
 
 def per_device(density, speed, codes, obstacle):
@@ -393,7 +416,6 @@
 
     fine_lines = (TILES, SPAN + 8, LANES)
     coarse_lines = (TILES_C, SPAN_C, LANES)
-    fine_cells, coarse_cells = (pltpu.VMEM((SPAN_C * n // 8, 8, LANES), f32) for n in (2 * TILES, TILES_C))
     result = pl.pallas_call(
         main_kernel,
         out_shape=jax.ShapeDtypeStruct((HEIGHT, TILES * LANES), f32),
@@ -402,19 +424,21 @@
             pltpu.VMEM(fine_lines, f32),
             pltpu.VMEM(fine_lines, f32),
             pltpu.VMEM(fine_lines, f32),
+            pltpu.VMEM(fine_lines, f32),
             pltpu.VMEM((8, *fine_lines), f32),
             pltpu.VMEM((3, *fine_lines), i32),
             pltpu.VMEM(fine_lines, f32),
-            fine_cells,
+            pltpu.VMEM((STAGES[0][1] * TILES, 8, LANES), f32),
             pltpu.VMEM(coarse_lines, f32),
             pltpu.VMEM((8, *coarse_lines), f32),
             pltpu.VMEM((3, *coarse_lines), i32),
             pltpu.VMEM(coarse_lines, f32),
-            coarse_cells,
-            coarse_cells,
+            pltpu.VMEM((2 * SPAN_C * TILES_C // 8, 8, LANES), f32),
             pltpu.VMEM(coarse_lines, f32),
-            pltpu.VMEM(coarse_lines, f32),
+            pltpu.VMEM((HEIGHT, TILES * LANES), f32),
+            pltpu.SemaphoreType.DMA((4,)),
         ],
+        out_specs=pl.BlockSpec(memory_space=pl.ANY),
         compiler_params=pltpu.CompilerParams(vmem_limit_bytes=32 * 1024 * 1024),
         name="parareal",
     )(own, crossed, paired)

time: 27.6 us -> 26.7 us (0.967)
  Pallas kernels: 18 us -> 17 us
    pallas_call x1, Pallas kernels: 15 us -> 14.1 us  [per_device(): pl.pallas_call(main_kernel, out_shape=jax.ShapeDtypeStruct((HEIGHT, TILES...]
where the time goes in v3:
time: 26.7 us; the launch traced here: 26.6 us
  Pallas kernels  17 us (64%)
  waiting for transfers between devices  6.55 us (25%)
  starting transfers between devices  2.94 us (11%)
    pallas_call x1, Pallas kernels, per_device(): pl.pallas_call(main_kernel, out_shape=jax.ShapeDtypeStruct((HEIGHT, TILES...  14.1 us
    ppermute x1, waiting for transfers between devices, per_device(): lax.ppermute(to_cross, 'strip', across + [(j, i) for i, j in across])  6.54 us
    ppermute x1, starting transfers between devices, per_device(): lax.ppermute(to_cross, 'strip', across + [(j, i) for i, j in across])  2.78 us
    pallas_call x1, Pallas kernels, per_device(): pl.pallas_call(own_kernel, out_shape=(pltpu.VMEM((TILES, 3 * HEIGHT, LANE...  1.88 us
    pallas_call x1, Pallas kernels, per_device(): pl.pallas_call(cross_kernel, out_shape=sent_shape, in_specs=[pl.BlockSpec...  1.06 us
  transfers between devices with their start and end apart: 2, of which 1 were waited for; matrix products, arithmetic and copies ran while one was open for 0% of the time, Pallas kernels for 7%

profile of v3, /device:TPU:223, one launch (start us, length us, event | category | flops | bytes accessed | tf_op | source)
XLA Modules:
  0.0 26.6 jit_solution(9866626431646420915)
XLA Ops:
  0.0 1.1 %cross.1 = f32[4,104,128]{2,1,0:T(8,128)S(1)} custom-call(f32[64,512]{1,0:T(8,128)} %density.3, f32[64,512]{1,0:T(8,128)} %speed.3, s32[64,512]{1,0:T(8,128)} %codes.3, s32[64,512]{1,0:T(8,128)} %obstacle.3), custom_call_target="tpu_custom_call" | custom-call | tf_op jit(solution)/shard_map/cross/pallas_call | solution.py:398
  1.1 2.8 %collective-permute-start = (f32[4,104,128]{2,1,0:T(8,128)S(1)}, f32[4,104,128]{2,1,0:T(8,128)S(1)}, u32[]{:S(2)}, u32[]{:S(2)}) collective-permute-start(f32[4,104,128]{2,1,0:T(8,128)S(1)} %cross.1), channel_id=1, source_target_pairs={{1,2},{3,4},{5,6},{7,8},{9,10},{11,12},{13,14},{15,16},{17,18},{19... | collective-permute-start | bytes 638984 | tf_op jit(solution)/shard_map/ppermute | solution.py:408
  3.9 1.9 %own.1 = (f32[4,192,128]{2,1,0:T(8,128)S(1)}, f32[4,104,128]{2,1,0:T(8,128)S(1)}) custom-call(f32[64,512]{1,0:T(8,128)} %density.3, f32[64,512]{1,0:T(8,128)} %speed.3, s32[64,512]{1,0:T(8,128)} %codes.3, s32[64,512]{1,0:T(8,128)} %obstacle.3), custom_call_target="tpu_custom_call" | custom-call | flops 10000000 | bytes 2000000 | tf_op jit(solution)/shard_map/own/pallas_call | solution.py:409
  5.8 0.2 collective-permute-start.1
  5.9 6.5 %collective-permute-done.crossed = f32[4,104,128]{2,1,0:T(8,128)S(1)} collective-permute-done((f32[4,104,128]{2,1,0:T(8,128)S(1)}, f32[4,104,128]{2,1,0:T(8,128)S(1)}, u32[]{:S(2)}, u32[]{:S(2)}) %collective-permute-start) | collective-permute-done | bytes 213024 | tf_op jit(solution)/shard_map/ppermute | solution.py:408
  12.5 0.0 collective-permute-done.1.paired
  12.5 14.1 %parareal.1 = f32[64,512]{1,0:T(8,128)} custom-call(f32[4,192,128]{2,1,0:T(8,128)S(1)} %get-tuple-element.7.own, f32[4,104,128]{2,1,0:T(8,128)S(1)} %collective-permute-done.crossed, f32[4,104,128]{2,1,0:T(8,128)S(1)} %collective-permute-done.1.paired), custom_call_target="tpu_custom_call" | custom-call | tf_op jit(solution)/shard_map/parareal/pallas_call | solution.py:419
Async XLA Ops:
  1.1 11.4 %collective-permute-start = (f32[4,104,128]{2,1,0:T(8,128)S(1)}, f32[4,104,128]{2,1,0:T(8,128)S(1)}, u32[]{:S(2)}, u32[]{:S(2)}) collective-permute-start(f32[4,104,128]{2,1,0:T(8,128)S(1)} %cross.1), channel_id=1, source_target_pairs={{1,2},{3,4},{5,6},{7,8},{9,10},{11,12},{13,14},{15,16},{17,18},{19... | collective-permute-start | bytes 638984 | tf_op jit(solution)/shard_map/ppermute | solution.py:408
  5.8 6.7 %collective-permute-start.1 = (f32[4,104,128]{2,1,0:T(8,128)S(1)}, f32[4,104,128]{2,1,0:T(8,128)S(1)}, u32[]{:S(2)}, u32[]{:S(2)}) collective-permute-start(f32[4,104,128]{2,1,0:T(8,128)S(1)} %get-tuple-element.8), channel_id=1, source_target_pairs={{0,1},{2,3},{4,5},{6,7},{8,9},{10,11},{12,13},{14,15},{16,17},{18,... | collective-permute-start | bytes 638984 | tf_op jit(solution)/shard_map/ppermute | solution.py:415

commit v4 on v3

--- a/solution.py
+++ b/solution.py
@@ -168,9 +168,12 @@
     return values[0]
 
 
+SIDES = [[d for d, (_, dc) in enumerate(OFFSETS) if dc == step] for step in (1, -1)]
+
+
 class Level:
-    def __init__(self, first, rows, tiles, rate, parts, bits, weight):
-        self.first, self.rows, self.tiles = first, rows, tiles
+    def __init__(self, first, rows, tiles, rate, parts, bits, weight, sides=None):
+        self.first, self.rows, self.tiles, self.sides = first, rows, tiles, sides
         self.rate, self.parts, self.bits, self.weight = rate, parts, bits, weight
 
     def at(self, r, t):
@@ -203,7 +206,14 @@
             masks = [code == float(d) for d in range(8)]
             self.put(self.rate, r, t, rate)
             for d, mask in enumerate(masks):
-                self.put(self.parts.at[d], r, t, jnp.where(mask, rate, 0.0))
+                part = jnp.where(mask, rate, 0.0)
+                self.put(self.parts.at[d], r, t, part)
+                if self.sides is None:
+                    continue
+                if t == self.tiles - 1 and d in SIDES[0]:
+                    self.sides[SIDES[0].index(d), self.line(r), :] = from_left(part)
+                if t == 0 and d in SIDES[1]:
+                    self.sides[3 + SIDES[1].index(d), self.line(r), :] = from_right(part)
             number = code.astype(jnp.int32)
             for n in range(3):
                 self.put(self.bits.at[n], r, t, number & (1 << n))
@@ -215,6 +225,9 @@
         sweep(self.rows, self.tiles, amounts_at, emit)
 
     def advance(self, rho, base=0):
+        (self.advance_rolling_sums if self.sides is None else self.advance_entering)(rho, base)
+
+    def advance_rolling_sums(self, rho, base):
         rows, tiles = self.rows, self.tiles
         field, room = {}, {}
 
@@ -247,6 +260,63 @@
 
         sweep(rows, tiles, amounts_at, emit)
 
+    def advance_entering(self, rho, base):
+        rows, tiles = self.rows, self.tiles
+        field, room, sums, entering = {}, {}, {}, {}
+
+        def load(r):
+            for t in range(tiles):
+                field[r, t] = rho[base + self.at(r, t)]
+                room[r, t] = (1.0 - field[r, t]) * self.get(self.weight, r, t)
+            field[r, -1] = from_left(field[r, tiles - 1])
+            field[r, tiles] = from_right(field[r, 0])
+            room[r, -1] = from_left(room[r, tiles - 1])
+            room[r, tiles] = from_right(room[r, 0])
+
+        def add(target, key, value):
+            target[key] = target[key] + value if key in target else value
+
+        def finish(r):
+            add(sums, (r, 0), room[r, 0] * entering.pop((r, 0)))
+            add(sums, (r, tiles - 1), room[r, tiles - 1] * entering.pop((r, 1)))
+            for t in range(tiles):
+                rho[base + self.at(r, t)] = sums.pop((r, t))
+
+        for r in range(rows):
+            needed = [row for row in (r - 1, r, r + 1) if 0 <= row < rows] + [rows - 1] * (r == 0)
+            for row in needed:
+                if (row, 0) not in room:
+                    load(row)
+            if r == 0:
+                for t in range(-1, tiles + 1):
+                    room[-1, t] = from_above(room[rows - 1, t])
+            if r == rows - 1:
+                for t in range(-1, tiles + 1):
+                    room[rows, t] = from_below(room[0, t])
+            for t in (*range(1, tiles - 1), 0, tiles - 1):
+                bits = [self.get(self.bits.at[n], r, t) != 0 for n in range(3)]
+                leaving = picked(bits, [room[r + dr, t + dc] for dr, dc in OFFSETS])
+                share = field[r, t] * leaving
+                add(sums, (r, t), field[r, t] - self.get(self.rate, r, t) * share)
+                for d, (dr, dc) in enumerate(OFFSETS):
+                    if 0 <= t + dc < tiles:
+                        add(sums, (r + dr, t + dc), self.get(self.parts.at[d], r, t) * share)
+            for side, directions in enumerate(SIDES):
+                for i, d in enumerate(directions):
+                    pushed = self.sides[3 * side + i, self.line(r), :] * field[r, (-1, tiles)[side]]
+                    add(entering, (r + OFFSETS[d][0], side), pushed)
+            for row, target, moved in ((rows - 1, 0, from_above), (0, rows - 1, from_below)):
+                if r == row:
+                    beyond = rows if row else -1
+                    for t in range(tiles):
+                        add(sums, (target, t), moved(sums.pop((beyond, t))))
+                    for side in range(2):
+                        add(entering, (target, side), moved(entering.pop((beyond, side))))
+            if r >= 2:
+                finish(r - 1)
+        finish(rows - 1)
+        finish(0)
+
 
 def halved(coarse, lines, change=lambda tile: tile):
     def at(r, t):
@@ -265,7 +335,7 @@
 
 def main_kernel(
     own, crossed, paired, out, rate, code, start, sending, parts, bits, weight, rho,
-    crate, cparts, cbits, cweight, pair, last_guess, result, sems,
+    crate, cparts, cbits, cweight, csides, pair, last_guess, result, sems,
 ):
     even = lax.axis_index("strip") % 2 == 0
     fields = (rate, code, start)
@@ -300,7 +370,10 @@
             field[t, pl.ds(SPAN, 8), :] = zeros
 
     stages = [
-        (Level(*window, TILES, sending, parts, bits, weight), Level(*window_c, TILES_C, crate, cparts, cbits, cweight))
+        (
+            Level(*window, TILES, sending, parts, bits, weight),
+            Level(*window_c, TILES_C, crate, cparts, cbits, cweight, csides),
+        )
         for window, window_c in zip(STAGES, STAGES_C)
     ]
     fine, coarse = stages[0]
@@ -323,25 +396,22 @@
 
     half = SPAN_C * TILES_C // 8
 
-    @pl.when(n > 0)
-    def _():
-        for (r, t), value in halved(coarse, start).items():
-            pair[coarse.at(r, t)] = value
-
-        @pl.loop(0, CSTEPS)
-        def _(step):
-            coarse.advance(pair)
-
-        for r, t in coarse.cells():
-            coarse.put(last_guess, r, t, pair[coarse.at(r, t)])
-
+    for (r, t), value in halved(coarse, start).items():
+        pair[coarse.at(r, t)] = value
     for r, t in fine.cells():
         rho[fine.at(r, t)] = fine.get(start, r, t)
 
-    @pl.loop(0, FINE)
+    @pl.loop(0, CSTEPS)
     def _(step):
         fine.advance(rho)
-
+        coarse.advance(pair)
+
+    @pl.loop(CSTEPS, FINE)
+    def _(step):
+        fine.advance(rho)
+
+    for r, t in coarse.cells():
+        coarse.put(last_guess, r, t, pair[coarse.at(r, t)])
     for r, t in fine.cells():
         fine.put(start, r, t, rho[fine.at(r, t)])
 
@@ -361,11 +431,7 @@
             @pl.loop(0, FINE)
             def _(step):
                 fine.advance(rho)
-
-            @pl.loop(0, CSTEPS)
-            def _(step):
-                coarse.advance(pair)
-                coarse.advance(pair, half)
+                coarse.advance(pair, half * (step // CSTEPS))
 
             for r, t in coarse.cells():
                 value = pair[coarse.at(r, t)]
@@ -433,6 +499,7 @@
             pltpu.VMEM((8, *coarse_lines), f32),
             pltpu.VMEM((3, *coarse_lines), i32),
             pltpu.VMEM(coarse_lines, f32),
+            pltpu.VMEM((6, *coarse_lines[1:]), f32),
             pltpu.VMEM((2 * SPAN_C * TILES_C // 8, 8, LANES), f32),
             pltpu.VMEM(coarse_lines, f32),
             pltpu.VMEM((HEIGHT, TILES * LANES), f32),

time: 26.7 us -> 25.5 us (0.955)
  Pallas kernels: 17 us -> 15.8 us
    pallas_call x1, Pallas kernels: 14.1 us -> 12.8 us  [per_device(): pl.pallas_call(main_kernel, out_shape=jax.ShapeDtypeStruct((HEIGHT, TILES...]
where the time goes in v4:
time: 25.5 us; the launch traced here: 25.3 us
  Pallas kernels  15.8 us (62%)
  waiting for transfers between devices  6.55 us (26%)
  starting transfers between devices  2.94 us (12%)
    pallas_call x1, Pallas kernels, per_device(): pl.pallas_call(main_kernel, out_shape=jax.ShapeDtypeStruct((HEIGHT, TILES...  12.8 us
    ppermute x1, waiting for transfers between devices, per_device(): lax.ppermute(to_cross, 'strip', across + [(j, i) for i, j in across])  6.54 us
    ppermute x1, starting transfers between devices, per_device(): lax.ppermute(to_cross, 'strip', across + [(j, i) for i, j in across])  2.78 us
    pallas_call x1, Pallas kernels, per_device(): pl.pallas_call(own_kernel, out_shape=(pltpu.VMEM((TILES, 3 * HEIGHT, LANE...  1.88 us
    pallas_call x1, Pallas kernels, per_device(): pl.pallas_call(cross_kernel, out_shape=sent_shape, in_specs=[pl.BlockSpec...  1.06 us
  transfers between devices with their start and end apart: 2, of which 1 were waited for; matrix products, arithmetic and copies ran while one was open for 0% of the time, Pallas kernels for 7%

profile of v4, /device:TPU:223, one launch (start us, length us, event | category | flops | bytes accessed | tf_op | source)
XLA Modules:
  0.0 25.3 jit_solution(1218447511757840232)
XLA Ops:
  0.0 1.1 %cross.1 = f32[4,104,128]{2,1,0:T(8,128)S(1)} custom-call(f32[64,512]{1,0:T(8,128)} %density.3, f32[64,512]{1,0:T(8,128)} %speed.3, s32[64,512]{1,0:T(8,128)} %codes.3, s32[64,512]{1,0:T(8,128)} %obstacle.3), custom_call_target="tpu_custom_call" | custom-call | tf_op jit(solution)/shard_map/cross/pallas_call | solution.py:464
  1.1 2.8 %collective-permute-start = (f32[4,104,128]{2,1,0:T(8,128)S(1)}, f32[4,104,128]{2,1,0:T(8,128)S(1)}, u32[]{:S(2)}, u32[]{:S(2)}) collective-permute-start(f32[4,104,128]{2,1,0:T(8,128)S(1)} %cross.1), channel_id=1, source_target_pairs={{1,2},{3,4},{5,6},{7,8},{9,10},{11,12},{13,14},{15,16},{17,18},{19... | collective-permute-start | bytes 638984 | tf_op jit(solution)/shard_map/ppermute | solution.py:474
  3.9 1.9 %own.1 = (f32[4,192,128]{2,1,0:T(8,128)S(1)}, f32[4,104,128]{2,1,0:T(8,128)S(1)}) custom-call(f32[64,512]{1,0:T(8,128)} %density.3, f32[64,512]{1,0:T(8,128)} %speed.3, s32[64,512]{1,0:T(8,128)} %codes.3, s32[64,512]{1,0:T(8,128)} %obstacle.3), custom_call_target="tpu_custom_call" | custom-call | flops 10000000 | bytes 2000000 | tf_op jit(solution)/shard_map/own/pallas_call | solution.py:475
  5.8 0.2 collective-permute-start.1
  5.9 6.5 %collective-permute-done.crossed = f32[4,104,128]{2,1,0:T(8,128)S(1)} collective-permute-done((f32[4,104,128]{2,1,0:T(8,128)S(1)}, f32[4,104,128]{2,1,0:T(8,128)S(1)}, u32[]{:S(2)}, u32[]{:S(2)}) %collective-permute-start) | collective-permute-done | bytes 213024 | tf_op jit(solution)/shard_map/ppermute | solution.py:474
  12.5 0.0 collective-permute-done.1.paired
  12.5 12.8 %parareal.1 = f32[64,512]{1,0:T(8,128)} custom-call(f32[4,192,128]{2,1,0:T(8,128)S(1)} %get-tuple-element.7.own, f32[4,104,128]{2,1,0:T(8,128)S(1)} %collective-permute-done.crossed, f32[4,104,128]{2,1,0:T(8,128)S(1)} %collective-permute-done.1.paired), custom_call_target="tpu_custom_call" | custom-call | tf_op jit(solution)/shard_map/parareal/pallas_call | solution.py:485
Async XLA Ops:
  1.1 11.4 %collective-permute-start = (f32[4,104,128]{2,1,0:T(8,128)S(1)}, f32[4,104,128]{2,1,0:T(8,128)S(1)}, u32[]{:S(2)}, u32[]{:S(2)}) collective-permute-start(f32[4,104,128]{2,1,0:T(8,128)S(1)} %cross.1), channel_id=1, source_target_pairs={{1,2},{3,4},{5,6},{7,8},{9,10},{11,12},{13,14},{15,16},{17,18},{19... | collective-permute-start | bytes 638984 | tf_op jit(solution)/shard_map/ppermute | solution.py:474
  5.8 6.7 %collective-permute-start.1 = (f32[4,104,128]{2,1,0:T(8,128)S(1)}, f32[4,104,128]{2,1,0:T(8,128)S(1)}, u32[]{:S(2)}, u32[]{:S(2)}) collective-permute-start(f32[4,104,128]{2,1,0:T(8,128)S(1)} %get-tuple-element.8), channel_id=1, source_target_pairs={{0,1},{2,3},{4,5},{6,7},{8,9},{10,11},{12,13},{14,15},{16,17},{18,... | collective-permute-start | bytes 638984 | tf_op jit(solution)/shard_map/ppermute | solution.py:481

commit v5 on v4

--- a/solution.py
+++ b/solution.py
@@ -20,7 +20,7 @@
 SENT = 3 * HALO + 8
 STAGES = ((7, 17), (16, 14), (24, 12), (32, 10))
 STAGES_C = ((3, 9), (8, 7), (12, 6), (16, 5))
-SPAN_C = (SPAN + 8) // 2
+LINES, LINES_C = 168, 88
 
 
 def lane_ids():
@@ -394,7 +394,7 @@
 
     n = lax.axis_index("tm")
 
-    half = SPAN_C * TILES_C // 8
+    half = STAGES_C[0][1] * TILES_C
 
     for (r, t), value in halved(coarse, start).items():
         pair[coarse.at(r, t)] = value
@@ -480,8 +480,8 @@
     )(*args)
     paired = lax.ppermute(to_pair, "strip", within + [(j, i) for i, j in within])
 
-    fine_lines = (TILES, SPAN + 8, LANES)
-    coarse_lines = (TILES_C, SPAN_C, LANES)
+    fine_lines = (TILES, LINES, LANES)
+    coarse_lines = (TILES_C, LINES_C, LANES)
     result = pl.pallas_call(
         main_kernel,
         out_shape=jax.ShapeDtypeStruct((HEIGHT, TILES * LANES), f32),
@@ -500,7 +500,7 @@
             pltpu.VMEM((3, *coarse_lines), i32),
             pltpu.VMEM(coarse_lines, f32),
             pltpu.VMEM((6, *coarse_lines[1:]), f32),
-            pltpu.VMEM((2 * SPAN_C * TILES_C // 8, 8, LANES), f32),
+            pltpu.VMEM((2 * STAGES_C[0][1] * TILES_C, 8, LANES), f32),
             pltpu.VMEM(coarse_lines, f32),
             pltpu.VMEM((HEIGHT, TILES * LANES), f32),
             pltpu.SemaphoreType.DMA((4,)),

time: 25.5 us -> 25.4 us (level)
  no operation moved by 1% of the time
where the time goes in v5:
time: 25.4 us; the launch traced here: 25.3 us
  Pallas kernels  15.8 us (62%)
  waiting for transfers between devices  6.55 us (26%)
  starting transfers between devices  2.94 us (12%)
    pallas_call x1, Pallas kernels, per_device(): pl.pallas_call(main_kernel, out_shape=jax.ShapeDtypeStruct((HEIGHT, TILES...  12.8 us
    ppermute x1, waiting for transfers between devices, per_device(): lax.ppermute(to_cross, 'strip', across + [(j, i) for i, j in across])  6.54 us
    ppermute x1, starting transfers between devices, per_device(): lax.ppermute(to_cross, 'strip', across + [(j, i) for i, j in across])  2.78 us
    pallas_call x1, Pallas kernels, per_device(): pl.pallas_call(own_kernel, out_shape=(pltpu.VMEM((TILES, 3 * HEIGHT, LANE...  1.88 us
    pallas_call x1, Pallas kernels, per_device(): pl.pallas_call(cross_kernel, out_shape=sent_shape, in_specs=[pl.BlockSpec...  1.06 us
  transfers between devices with their start and end apart: 2, of which 1 were waited for; matrix products, arithmetic and copies ran while one was open for 0% of the time, Pallas kernels for 7%

profile of v5, /device:TPU:223, one launch (start us, length us, event | category | flops | bytes accessed | tf_op | source)
XLA Modules:
  0.0 25.3 jit_solution(5617609282827864696)
XLA Ops:
  0.0 1.1 %cross.1 = f32[4,104,128]{2,1,0:T(8,128)S(1)} custom-call(f32[64,512]{1,0:T(8,128)} %density.3, f32[64,512]{1,0:T(8,128)} %speed.3, s32[64,512]{1,0:T(8,128)} %codes.3, s32[64,512]{1,0:T(8,128)} %obstacle.3), custom_call_target="tpu_custom_call" | custom-call | tf_op jit(solution)/shard_map/cross/pallas_call | solution.py:464
  1.1 2.8 %collective-permute-start = (f32[4,104,128]{2,1,0:T(8,128)S(1)}, f32[4,104,128]{2,1,0:T(8,128)S(1)}, u32[]{:S(2)}, u32[]{:S(2)}) collective-permute-start(f32[4,104,128]{2,1,0:T(8,128)S(1)} %cross.1), channel_id=1, source_target_pairs={{1,2},{3,4},{5,6},{7,8},{9,10},{11,12},{13,14},{15,16},{17,18},{19... | collective-permute-start | bytes 638984 | tf_op jit(solution)/shard_map/ppermute | solution.py:474
  3.9 1.9 %own.1 = (f32[4,192,128]{2,1,0:T(8,128)S(1)}, f32[4,104,128]{2,1,0:T(8,128)S(1)}) custom-call(f32[64,512]{1,0:T(8,128)} %density.3, f32[64,512]{1,0:T(8,128)} %speed.3, s32[64,512]{1,0:T(8,128)} %codes.3, s32[64,512]{1,0:T(8,128)} %obstacle.3), custom_call_target="tpu_custom_call" | custom-call | flops 10000000 | bytes 2000000 | tf_op jit(solution)/shard_map/own/pallas_call | solution.py:475
  5.8 0.2 collective-permute-start.1
  5.9 6.5 %collective-permute-done.crossed = f32[4,104,128]{2,1,0:T(8,128)S(1)} collective-permute-done((f32[4,104,128]{2,1,0:T(8,128)S(1)}, f32[4,104,128]{2,1,0:T(8,128)S(1)}, u32[]{:S(2)}, u32[]{:S(2)}) %collective-permute-start) | collective-permute-done | bytes 213024 | tf_op jit(solution)/shard_map/ppermute | solution.py:474
  12.5 0.0 collective-permute-done.1.paired
  12.5 12.8 %parareal.1 = f32[64,512]{1,0:T(8,128)} custom-call(f32[4,192,128]{2,1,0:T(8,128)S(1)} %get-tuple-element.7.own, f32[4,104,128]{2,1,0:T(8,128)S(1)} %collective-permute-done.crossed, f32[4,104,128]{2,1,0:T(8,128)S(1)} %collective-permute-done.1.paired), custom_call_target="tpu_custom_call" | custom-call | tf_op jit(solution)/shard_map/parareal/pallas_call | solution.py:485
Async XLA Ops:
  1.1 11.4 %collective-permute-start = (f32[4,104,128]{2,1,0:T(8,128)S(1)}, f32[4,104,128]{2,1,0:T(8,128)S(1)}, u32[]{:S(2)}, u32[]{:S(2)}) collective-permute-start(f32[4,104,128]{2,1,0:T(8,128)S(1)} %cross.1), channel_id=1, source_target_pairs={{1,2},{3,4},{5,6},{7,8},{9,10},{11,12},{13,14},{15,16},{17,18},{19... | collective-permute-start | bytes 638984 | tf_op jit(solution)/shard_map/ppermute | solution.py:474
  5.8 6.7 %collective-permute-start.1 = (f32[4,104,128]{2,1,0:T(8,128)S(1)}, f32[4,104,128]{2,1,0:T(8,128)S(1)}, u32[]{:S(2)}, u32[]{:S(2)}) collective-permute-start(f32[4,104,128]{2,1,0:T(8,128)S(1)} %get-tuple-element.8), channel_id=1, source_target_pairs={{0,1},{2,3},{4,5},{6,7},{8,9},{10,11},{12,13},{14,15},{16,17},{18,... | collective-permute-start | bytes 638984 | tf_op jit(solution)/shard_map/ppermute | solution.py:481

commit v6 on v5

--- a/solution.py
+++ b/solution.py
@@ -31,31 +31,31 @@
     return lax.broadcasted_iota(jnp.int32, (8, LANES), 0)
 
 
+def exchange_blocks(tiles):
+    lane = lane_ids()
+
+    def swap(first, second, width):
+        low = lane % (2 * width) < width
+        return (
+            jnp.where(low, first, pltpu.roll(second, width, 1)),
+            jnp.where(low, pltpu.roll(first, LANES - width, 1), second),
+        )
+
+    a, b, c, d = tiles
+    (a, c), (b, d) = swap(a, c, 64), swap(b, d, 64)
+    return [*swap(a, b, 32), *swap(c, d, 32)]
+
+
 def interleave(tiles):
     lane = lane_ids()
-    result = []
-    for t in range(TILES):
-        index = (lane * TILES + t) % LANES
-        picked = [jnp.take_along_axis(tile, index, axis=1) for tile in tiles]
-        merged = picked[3]
-        for j in (2, 1, 0):
-            merged = jnp.where(lane < 32 * (j + 1), picked[j], merged)
-        result.append(merged)
-    return result
+    index = TILES * (lane % 32) + lane // 32
+    return exchange_blocks([jnp.take_along_axis(tile, index, axis=1) for tile in tiles])
 
 
 def deinterleave(tiles):
     lane = lane_ids()
-    part = lane % TILES
-    result = []
-    for j in range(TILES):
-        index = lane // TILES + 32 * j
-        picked = [jnp.take_along_axis(tile, index, axis=1) for tile in tiles]
-        merged = picked[3]
-        for t in (2, 1, 0):
-            merged = jnp.where(part == t, picked[t], merged)
-        result.append(merged)
-    return result
+    index = 32 * (lane % TILES) + lane // TILES
+    return [jnp.take_along_axis(tile, index, axis=1) for tile in exchange_blocks(tiles)]
 
 
 def products(density, speed, codes, obstacle, rows):

time: 25.4 us -> 25.3 us (level)
  waiting for transfers between devices: 6.55 us -> 5.91 us
  Pallas kernels: 15.8 us -> 16.3 us
    pallas_call x1, Pallas kernels: 1.88 us -> 2.52 us  [per_device(): pl.pallas_call(own_kernel, out_shape=(pltpu.VMEM((TILES, 3 * HEIGHT, LANE...]
    ppermute x1, waiting for transfers between devices: 6.54 us -> 5.91 us  [per_device(): lax.ppermute(to_cross, 'strip', across + [(j, i) for i, j in across])]
  transfers between devices with their start and end apart: 2 -> 2, of which waited for: 1 -> 1; matrix products, arithmetic and copies ran while one was open for 0% -> 0% of each run, Pallas kernels for 7% -> 10%
where the time goes in v6:
time: 25.3 us; the launch traced here: 25.2 us
  Pallas kernels  16.3 us (64%)
  waiting for transfers between devices  5.91 us (23%)
  starting transfers between devices  2.94 us (12%)
    pallas_call x1, Pallas kernels, per_device(): pl.pallas_call(main_kernel, out_shape=jax.ShapeDtypeStruct((HEIGHT, TILES...  12.7 us
    ppermute x1, waiting for transfers between devices, per_device(): lax.ppermute(to_cross, 'strip', across + [(j, i) for i, j in across])  5.91 us
    ppermute x1, starting transfers between devices, per_device(): lax.ppermute(to_cross, 'strip', across + [(j, i) for i, j in across])  2.78 us
    pallas_call x1, Pallas kernels, per_device(): pl.pallas_call(own_kernel, out_shape=(pltpu.VMEM((TILES, 3 * HEIGHT, LANE...  2.52 us
    pallas_call x1, Pallas kernels, per_device(): pl.pallas_call(cross_kernel, out_shape=sent_shape, in_specs=[pl.BlockSpec...  1.06 us
  transfers between devices with their start and end apart: 2, of which 1 were waited for; matrix products, arithmetic and copies ran while one was open for 0% of the time, Pallas kernels for 10%

profile of v6, /device:TPU:223, one launch (start us, length us, event | category | flops | bytes accessed | tf_op | source)
XLA Modules:
  0.0 25.2 jit_solution(10679664753385363549)
XLA Ops:
  0.0 1.1 %cross.1 = f32[4,104,128]{2,1,0:T(8,128)S(1)} custom-call(f32[64,512]{1,0:T(8,128)} %density.3, f32[64,512]{1,0:T(8,128)} %speed.3, s32[64,512]{1,0:T(8,128)} %codes.3, s32[64,512]{1,0:T(8,128)} %obstacle.3), custom_call_target="tpu_custom_call" | custom-call | tf_op jit(solution)/shard_map/cross/pallas_call | solution.py:464
  1.1 2.8 %collective-permute-start = (f32[4,104,128]{2,1,0:T(8,128)S(1)}, f32[4,104,128]{2,1,0:T(8,128)S(1)}, u32[]{:S(2)}, u32[]{:S(2)}) collective-permute-start(f32[4,104,128]{2,1,0:T(8,128)S(1)} %cross.1), channel_id=1, source_target_pairs={{1,2},{3,4},{5,6},{7,8},{9,10},{11,12},{13,14},{15,16},{17,18},{19... | collective-permute-start | bytes 638984 | tf_op jit(solution)/shard_map/ppermute | solution.py:474
  3.9 2.5 %own.1 = (f32[4,192,128]{2,1,0:T(8,128)S(1)}, f32[4,104,128]{2,1,0:T(8,128)S(1)}) custom-call(f32[64,512]{1,0:T(8,128)} %density.3, f32[64,512]{1,0:T(8,128)} %speed.3, s32[64,512]{1,0:T(8,128)} %codes.3, s32[64,512]{1,0:T(8,128)} %obstacle.3), custom_call_target="tpu_custom_call" | custom-call | flops 10000000 | bytes 2000000 | tf_op jit(solution)/shard_map/own/pallas_call | solution.py:475
  6.4 0.2 collective-permute-start.1
  6.5 5.9 %collective-permute-done.crossed = f32[4,104,128]{2,1,0:T(8,128)S(1)} collective-permute-done((f32[4,104,128]{2,1,0:T(8,128)S(1)}, f32[4,104,128]{2,1,0:T(8,128)S(1)}, u32[]{:S(2)}, u32[]{:S(2)}) %collective-permute-start) | collective-permute-done | bytes 213024 | tf_op jit(solution)/shard_map/ppermute | solution.py:474
  12.5 0.0 collective-permute-done.1.paired
  12.5 12.7 %parareal.1 = f32[64,512]{1,0:T(8,128)} custom-call(f32[4,192,128]{2,1,0:T(8,128)S(1)} %get-tuple-element.7.own, f32[4,104,128]{2,1,0:T(8,128)S(1)} %collective-permute-done.crossed, f32[4,104,128]{2,1,0:T(8,128)S(1)} %collective-permute-done.1.paired), custom_call_target="tpu_custom_call" | custom-call | tf_op jit(solution)/shard_map/parareal/pallas_call | solution.py:485
Async XLA Ops:
  1.1 11.4 %collective-permute-start = (f32[4,104,128]{2,1,0:T(8,128)S(1)}, f32[4,104,128]{2,1,0:T(8,128)S(1)}, u32[]{:S(2)}, u32[]{:S(2)}) collective-permute-start(f32[4,104,128]{2,1,0:T(8,128)S(1)} %cross.1), channel_id=1, source_target_pairs={{1,2},{3,4},{5,6},{7,8},{9,10},{11,12},{13,14},{15,16},{17,18},{19... | collective-permute-start | bytes 638984 | tf_op jit(solution)/shard_map/ppermute | solution.py:474
  6.4 6.1 %collective-permute-start.1 = (f32[4,104,128]{2,1,0:T(8,128)S(1)}, f32[4,104,128]{2,1,0:T(8,128)S(1)}, u32[]{:S(2)}, u32[]{:S(2)}) collective-permute-start(f32[4,104,128]{2,1,0:T(8,128)S(1)} %get-tuple-element.8), channel_id=1, source_target_pairs={{0,1},{2,3},{4,5},{6,7},{8,9},{10,11},{12,13},{14,15},{16,17},{18,... | collective-permute-start | bytes 638984 | tf_op jit(solution)/shard_map/ppermute | solution.py:481

commit v7 on v6

--- a/solution.py
+++ b/solution.py
@@ -50,6 +50,19 @@
     lane = lane_ids()
     index = TILES * (lane % 32) + lane // 32
     return exchange_blocks([jnp.take_along_axis(tile, index, axis=1) for tile in tiles])
+
+
+def interleave_by_gathers(tiles):
+    lane = lane_ids()
+    result = []
+    for t in range(TILES):
+        index = (lane * TILES + t) % LANES
+        picked = [jnp.take_along_axis(tile, index, axis=1) for tile in tiles]
+        merged = picked[3]
+        for j in (2, 1, 0):
+            merged = jnp.where(lane < 32 * (j + 1), picked[j], merged)
+        result.append(merged)
+    return result
 
 
 def deinterleave(tiles):
@@ -101,7 +114,7 @@
     for block in range(HEIGHT // 8):
         fields = products(density, speed, codes, obstacle, pl.ds(8 * block, 8))
         for field, tiles in enumerate(fields):
-            for t, value in enumerate(interleave(tiles)):
+            for t, value in enumerate(interleave_by_gathers(tiles)):
                 own[t, pl.ds(HEIGHT * field + 8 * block, 8), :] = value
     for t in range(TILES):
         for field in range(3):

time: 25.3 us -> 25.3 us (level)
  waiting for transfers between devices: 5.91 us -> 6.55 us
  Pallas kernels: 16.3 us -> 15.7 us
    pallas_call x1, Pallas kernels: 2.52 us -> 1.88 us  [per_device(): pl.pallas_call(own_kernel, out_shape=(pltpu.VMEM((TILES, 3 * HEIGHT, LANE...]
    ppermute x1, waiting for transfers between devices: 5.91 us -> 6.54 us  [per_device(): lax.ppermute(to_cross, 'strip', across + [(j, i) for i, j in across])]
  transfers between devices with their start and end apart: 2 -> 2, of which waited for: 1 -> 1; matrix products, arithmetic and copies ran while one was open for 0% -> 0% of each run, Pallas kernels for 10% -> 7%
where the time goes in v7:
time: 25.3 us; the launch traced here: 25.2 us
  Pallas kernels  15.7 us (62%)
  waiting for transfers between devices  6.55 us (26%)
  starting transfers between devices  2.94 us (12%)
    pallas_call x1, Pallas kernels, per_device(): pl.pallas_call(main_kernel, out_shape=jax.ShapeDtypeStruct((HEIGHT, TILES...  12.7 us
    ppermute x1, waiting for transfers between devices, per_device(): lax.ppermute(to_cross, 'strip', across + [(j, i) for i, j in across])  6.54 us
    ppermute x1, starting transfers between devices, per_device(): lax.ppermute(to_cross, 'strip', across + [(j, i) for i, j in across])  2.78 us
    pallas_call x1, Pallas kernels, per_device(): pl.pallas_call(own_kernel, out_shape=(pltpu.VMEM((TILES, 3 * HEIGHT, LANE...  1.88 us
    pallas_call x1, Pallas kernels, per_device(): pl.pallas_call(cross_kernel, out_shape=sent_shape, in_specs=[pl.BlockSpec...  1.06 us
  transfers between devices with their start and end apart: 2, of which 1 were waited for; matrix products, arithmetic and copies ran while one was open for 0% of the time, Pallas kernels for 7%

profile of v7, /device:TPU:223, one launch (start us, length us, event | category | flops | bytes accessed | tf_op | source)
XLA Modules:
  0.0 25.2 jit_solution(8661266269104736530)
XLA Ops:
  0.0 1.1 %cross.1 = f32[4,104,128]{2,1,0:T(8,128)S(1)} custom-call(f32[64,512]{1,0:T(8,128)} %density.3, f32[64,512]{1,0:T(8,128)} %speed.3, s32[64,512]{1,0:T(8,128)} %codes.3, s32[64,512]{1,0:T(8,128)} %obstacle.3), custom_call_target="tpu_custom_call" | custom-call | tf_op jit(solution)/shard_map/cross/pallas_call | solution.py:477
  1.1 2.8 %collective-permute-start = (f32[4,104,128]{2,1,0:T(8,128)S(1)}, f32[4,104,128]{2,1,0:T(8,128)S(1)}, u32[]{:S(2)}, u32[]{:S(2)}) collective-permute-start(f32[4,104,128]{2,1,0:T(8,128)S(1)} %cross.1), channel_id=1, source_target_pairs={{1,2},{3,4},{5,6},{7,8},{9,10},{11,12},{13,14},{15,16},{17,18},{19... | collective-permute-start | bytes 638984 | tf_op jit(solution)/shard_map/ppermute | solution.py:487
  3.9 1.9 %own.1 = (f32[4,192,128]{2,1,0:T(8,128)S(1)}, f32[4,104,128]{2,1,0:T(8,128)S(1)}) custom-call(f32[64,512]{1,0:T(8,128)} %density.3, f32[64,512]{1,0:T(8,128)} %speed.3, s32[64,512]{1,0:T(8,128)} %codes.3, s32[64,512]{1,0:T(8,128)} %obstacle.3), custom_call_target="tpu_custom_call" | custom-call | flops 10000000 | bytes 2000000 | tf_op jit(solution)/shard_map/own/pallas_call | solution.py:488
  5.8 0.2 collective-permute-start.1
  5.9 6.5 %collective-permute-done.crossed = f32[4,104,128]{2,1,0:T(8,128)S(1)} collective-permute-done((f32[4,104,128]{2,1,0:T(8,128)S(1)}, f32[4,104,128]{2,1,0:T(8,128)S(1)}, u32[]{:S(2)}, u32[]{:S(2)}) %collective-permute-start) | collective-permute-done | bytes 213024 | tf_op jit(solution)/shard_map/ppermute | solution.py:487
  12.5 0.0 collective-permute-done.1.paired
  12.5 12.7 %parareal.1 = f32[64,512]{1,0:T(8,128)} custom-call(f32[4,192,128]{2,1,0:T(8,128)S(1)} %get-tuple-element.7.own, f32[4,104,128]{2,1,0:T(8,128)S(1)} %collective-permute-done.crossed, f32[4,104,128]{2,1,0:T(8,128)S(1)} %collective-permute-done.1.paired), custom_call_target="tpu_custom_call" | custom-call | tf_op jit(solution)/shard_map/parareal/pallas_call | solution.py:498
Async XLA Ops:
  1.1 11.4 %collective-permute-start = (f32[4,104,128]{2,1,0:T(8,128)S(1)}, f32[4,104,128]{2,1,0:T(8,128)S(1)}, u32[]{:S(2)}, u32[]{:S(2)}) collective-permute-start(f32[4,104,128]{2,1,0:T(8,128)S(1)} %cross.1), channel_id=1, source_target_pairs={{1,2},{3,4},{5,6},{7,8},{9,10},{11,12},{13,14},{15,16},{17,18},{19... | collective-permute-start | bytes 638984 | tf_op jit(solution)/shard_map/ppermute | solution.py:487
  5.8 6.7 %collective-permute-start.1 = (f32[4,104,128]{2,1,0:T(8,128)S(1)}, f32[4,104,128]{2,1,0:T(8,128)S(1)}, u32[]{:S(2)}, u32[]{:S(2)}) collective-permute-start(f32[4,104,128]{2,1,0:T(8,128)S(1)} %get-tuple-element.8), channel_id=1, source_target_pairs={{0,1},{2,3},{4,5},{6,7},{8,9},{10,11},{12,13},{14,15},{16,17},{18,... | collective-permute-start | bytes 638984 | tf_op jit(solution)/shard_map/ppermute | solution.py:494
